TPU v7x, 512 devices: a whole 4x4x16 slice. The times are simulated.
512 devices in a mesh: col: 64 (over z, x), wa: 8 (over y, core).
Axes of the slice: x: 4, y: 4, z: 16, core: 2. Of those that a mesh axis runs over, the one named last changes fastest.
Arguments:
- visibilities: bfloat16 [64, 8, 64, 2, 128], P('col', 'wa'), may hold values from -6 to 6
- visibility_uv_offsets: bfloat16 [64, 8, 64, 2, 128], P('col', 'wa'), may hold values from -16 to 16
- block_owner_index: int32 [64, 8, 64, 1], P('col', 'wa'), may hold values from 0 to 63; in each aligned block of 64 rows (0 to 63, 64 to 127, ..., all dimensions but the last counted through in order) at most 2 rows name the same one
- block_cell_number: int32 [64, 8, 64], P('col', 'wa'), may hold values from 0 to 1023
- live_counts: int32 [64, 8], P('col', 'wa'), may hold values from 48 to 64, as said below
- touch_lists: int32 [128, 12], P('col'), may hold values from -1 to 15, as said below
Outputs:
- facets: float32 [1024, 128], P(('col', 'wa'))
Inputs may be any that keep to these rules, and one draw needn't show every extreme that they name: `block_owner_index`: on every device at most 2 of its 64 block slots, live or not, name one owner; on some device one owner is named exactly 2 times. `live_counts`: the live slots of a device are its first ones; some device has all 64 live. `touch_lists`: row c names 6 to 12 different facets in its first places and -1 in the rest; some row names 12 facets.
All inputs are finite; a program needn't handle non-finite values.
Results may differ from a plain program's by a relative error of at most 0.0036.
Values may be sent and summed in bfloat16 or wider, within the bound.
No kernel may reach another device: no remote copies, remote signals or barrier semaphores. Data moves between devices by JAX's collectives and lax.ppermute only.
A program may use at most 64 MiB of HBM per device.

v0:
```python
import math

import jax
import jax.numpy as jnp
from jax import lax
from jax.sharding import PartitionSpec as P

S = 64
BLOCK_VISIBILITY = 128
RANGE_PLANES = 16
FACETS = 16
DEVICE_COLUMNS = 2
COLUMN_SUBGRIDS = 32
DEVICE_SLOTS = 64


FULL_TURN = 2.0 * math.pi
FIELD_WIDTH = 0.2
CELL_STEP = 0.37
WTERM_LIMIT = 4000.0
HIGHEST = lax.Precision.HIGHEST


def pixel_offsets(length):
    return jnp.arange(length).astype(jnp.float32) - jnp.float32(length // 2)


def phase_lag(length):
    direction = pixel_offsets(length) * (FIELD_WIDTH / length)
    radius = direction[:, None] ** 2 + direction[None, :] ** 2
    return -radius / (1.0 + jnp.sqrt(1.0 - radius))


def phasor_tables(coords, values):
    offsets = pixel_offsets(S) * (FULL_TURN / S)
    angle_u = coords[:, 0, :, None] * offsets
    angle_v = coords[:, 1, :, None] * offsets
    cosine_v = jnp.cos(angle_v)
    sine_v = jnp.sin(angle_v)
    real_part = values[:, 0, :, None]
    imag_part = values[:, 1, :, None]
    weighted_real = (real_part * cosine_v - imag_part * sine_v).astype(jnp.bfloat16)
    weighted_imag = (real_part * sine_v + imag_part * cosine_v).astype(jnp.bfloat16)
    left_table = jnp.concatenate(
        [jnp.cos(angle_u).astype(jnp.bfloat16), jnp.sin(angle_u).astype(jnp.bfloat16)], axis=1
    )
    upper_rows = jnp.concatenate([weighted_real, weighted_imag], axis=2)
    lower_rows = jnp.concatenate([-weighted_imag, weighted_real], axis=2)
    right_table = jnp.concatenate([upper_rows, lower_rows], axis=1)
    return (left_table, right_table)


def complex_times(operand, factor_real, factor_imag, extent):
    operand_real = operand[..., :extent]
    operand_imag = operand[..., extent:]
    return jnp.concatenate(
        [
            operand_real * factor_real - operand_imag * factor_imag,
            operand_real * factor_imag + operand_imag * factor_real,
        ],
        axis=-1,
    )


def shift_matrices(shifts):
    frequency = pixel_offsets(S) * (FULL_TURN / S)
    position = jnp.arange(S).astype(jnp.float32)
    left_angle = position[:, None] * frequency[None, :]
    right_angle = (position[None, :] + shifts[:, None])[..., None] * frequency
    cos_left = jnp.cos(left_angle)
    sin_left = jnp.sin(left_angle)
    cos_right = jnp.cos(right_angle)
    sin_right = jnp.sin(right_angle)
    real_part = jnp.einsum("xk,flk->fxl", cos_left, cos_right, precision=HIGHEST) + jnp.einsum(
        "xk,flk->fxl", sin_left, sin_right, precision=HIGHEST
    )
    imag_part = jnp.einsum("xk,flk->fxl", sin_left, cos_right, precision=HIGHEST) - jnp.einsum(
        "xk,flk->fxl", cos_left, sin_right, precision=HIGHEST
    )
    return (real_part / S, imag_part / S)


def facet_geometry():
    facet_ids = jnp.arange(FACETS)
    facet_column = (facet_ids % 4).astype(jnp.float32)
    facet_row = (facet_ids // 4).astype(jnp.float32)
    return (facet_column, facet_row)


def facet_weights(column_ids, row_ids, touched, column_total):
    facet_column, facet_row = facet_geometry()
    column_phase = (
        FULL_TURN
        * CELL_STEP
        * (column_ids - column_total / 2 + 0.5)[:, None]
        * ((facet_column - 1.5) / 4)[None, :]
    )
    row_phase = (
        FULL_TURN
        * CELL_STEP
        * (row_ids - COLUMN_SUBGRIDS / 2 + 0.5)[:, None]
        * ((facet_row - 1.5) / 4)[None, :]
    )
    angle_all = column_phase[:, None, :] + row_phase[None, :, :]
    return (jnp.cos(angle_all) * touched[:, None, :], jnp.sin(angle_all) * touched[:, None, :])


def combine_towers(weight_real, weight_imag, towers):
    swapped = jnp.concatenate([-towers[..., S:], towers[..., :S]], axis=-1)
    first_sum = jnp.einsum("cjf,cjlq->flq", weight_real, towers, precision=HIGHEST)
    second_sum = jnp.einsum("cjf,cjlq->flq", weight_imag, swapped, precision=HIGHEST)
    return first_sum + second_sum


def facet_image(summed):
    facet_column, facet_row = facet_geometry()
    shift_real, shift_imag = shift_matrices((facet_column + 0.5) / 4)
    other_real, other_imag = shift_matrices((facet_row + 0.5) / 4)
    swapped = jnp.concatenate([-summed[..., S:], summed[..., :S]], axis=-1)
    rotated = jnp.einsum("fxl,flq->fxq", shift_real, summed, precision=HIGHEST) + jnp.einsum(
        "fxl,flq->fxq", shift_imag, swapped, precision=HIGHEST
    )
    rotated_real = rotated[..., :S]
    rotated_imag = rotated[..., S:]
    result_real = jnp.einsum(
        "fxm,fym->fxy", rotated_real, other_real, precision=HIGHEST
    ) - jnp.einsum("fxm,fym->fxy", rotated_imag, other_imag, precision=HIGHEST)
    result_imag = jnp.einsum(
        "fxm,fym->fxy", rotated_real, other_imag, precision=HIGHEST
    ) + jnp.einsum("fxm,fym->fxy", rotated_imag, other_real, precision=HIGHEST)
    return jnp.concatenate([result_real, result_imag], axis=-1)


def shards(
    visibilities,
    visibility_uv_offsets,
    block_owner_index,
    block_cell_number,
    live_counts,
    touch_lists,
):
    column_count = lax.axis_size("col")
    wrange_count = lax.axis_size("wa")
    col_index = lax.axis_index("col")
    range_index = lax.axis_index("wa")
    values = visibilities[0, 0]
    coords = visibility_uv_offsets[0, 0]
    owner_indices = block_owner_index[0, 0, :, 0]
    cell_numbers = block_cell_number[0, 0]
    slot_total = values.shape[0]
    points = values.shape[2]
    capacity = 2 * slot_total // column_count
    live_rows = jnp.arange(slot_total) < live_counts[0, 0]
    values = jnp.where(live_rows[:, None, None], values, jnp.zeros_like(values))
    column_local = cell_numbers // (COLUMN_SUBGRIDS * RANGE_PLANES)
    row_local = cell_numbers // RANGE_PLANES % COLUMN_SUBGRIDS
    plane_local = cell_numbers % RANGE_PLANES
    chosen = (owner_indices[:, None] == jnp.arange(column_count)[None, :]).astype(jnp.int32)
    ranks = jnp.sum(chosen * (jnp.cumsum(chosen, axis=0) - 1), axis=1)
    destination = owner_indices * capacity + ranks
    position = jnp.arange(points)[None, :]
    label_row = jnp.where(
        position == 0,
        column_local[:, None],
        jnp.where(
            position == 1, row_local[:, None], jnp.where(position == 2, plane_local[:, None], 0)
        ),
    )
    label_row = label_row.astype(jnp.float32).astype(jnp.bfloat16)[:, None, :]
    packed = jnp.concatenate([values, coords, label_row], axis=1)
    outgoing = (
        jnp.zeros((column_count * capacity, 5, points), jnp.bfloat16).at[destination].set(packed)
    )
    incoming = lax.all_to_all(outgoing, "col", split_axis=0, concat_axis=0, tiled=True)
    block_data = incoming[:, 0:4]
    label_ids = incoming[:, 4, 0:3].astype(jnp.int32)
    tile_slots = 32
    tiles = block_data.reshape(-1, tile_slots, 4, points)
    label_tiles = label_ids.reshape(-1, tile_slots, 3)
    lag_field = phase_lag(S)
    plane_step = 2.0 * WTERM_LIMIT / (RANGE_PLANES * wrange_count)

    def grid_tile(towers_sum, tile_items):
        tile_data, tile_labels = tile_items
        left_table, right_table = phasor_tables(
            tile_data[:, 2:4].astype(jnp.float32), tile_data[:, 0:2].astype(jnp.float32)
        )
        block_grids = jnp.einsum(
            "nkl,nkq->nlq", left_table, right_table, preferred_element_type=jnp.float32
        )
        depth_ids = (range_index * RANGE_PLANES + tile_labels[:, 2]).astype(jnp.float32)
        plane_depths = -WTERM_LIMIT + (depth_ids + 0.5) * plane_step
        screen_angle = FULL_TURN * plane_depths[:, None, None] * lag_field
        contrib = complex_times(block_grids, jnp.cos(screen_angle), jnp.sin(screen_angle), S)
        flat_index = tile_labels[:, 0] * COLUMN_SUBGRIDS + tile_labels[:, 1]
        return (towers_sum.at[flat_index].add(contrib), None)

    towers = jnp.zeros((DEVICE_COLUMNS * COLUMN_SUBGRIDS, S, 2 * S), jnp.float32)
    towers, unused = lax.scan(grid_tile, towers, (tiles, label_tiles))
    flat_towers = towers.reshape(DEVICE_COLUMNS, COLUMN_SUBGRIDS, 2 * S * S)
    share = COLUMN_SUBGRIDS // wrange_count
    summed_towers = lax.psum(flat_towers, "wa")
    local_towers = lax.dynamic_slice_in_dim(summed_towers, range_index * share, share, 1).reshape(
        DEVICE_COLUMNS, share, S, 2 * S
    )
    first_row = range_index * share
    column_total = DEVICE_COLUMNS * column_count
    facet_ids = jnp.arange(FACETS)
    touched = jnp.any(touch_lists[:, :, None] == facet_ids[None, None, :], axis=1).astype(
        jnp.float32
    )
    row_ids = (first_row + jnp.arange(local_towers.shape[1])).astype(jnp.float32)
    column_ids = (col_index * DEVICE_COLUMNS + jnp.arange(DEVICE_COLUMNS)).astype(jnp.float32)
    weight_real, weight_imag = facet_weights(column_ids, row_ids, touched, column_total)
    summed = combine_towers(weight_real, weight_imag, local_towers)
    scale_multiplier = 1.0 / math.sqrt(
        BLOCK_VISIBILITY * column_count * wrange_count * DEVICE_SLOTS
    )
    facet_field = facet_image(summed) * scale_multiplier
    partial_rows = facet_field.reshape(FACETS * S, 2 * S)
    return lax.psum_scatter(partial_rows, ("col", "wa"), scatter_dimension=0, tiled=True)


def solution(mesh):
    placed = (
        P("col", "wa", None, None, None),
        P("col", "wa", None, None, None),
        P("col", "wa", None, None),
        P("col", "wa", None),
        P("col", "wa"),
        P("col", None),
    )
    return jax.shard_map(
        shards, mesh=mesh, in_specs=placed, out_specs=P(("col", "wa"), None), check_vma=False
    )
```

profile of v0, /device:TPU:1, one launch (start us, length us, event | category | flops | bytes accessed | tf_op | source)
XLA Modules:
  0.0 748.3 jit_solution(9776213602156367158)
XLA Ops:
  6.5 0.7 and_select_fusion
  7.9 0.7 fusion.84
  8.7 0.8 select_reduce_fusion
  9.5 0.7 fusion.117
  10.2 0.9 broadcast_select_fusion
  11.1 0.3 fusion.83
  11.4 0.9 pad_maximum_fusion.2
  12.3 0.7 broadcast_in_dim.66
  13.0 6.5 scatter_fusion.1
  19.5 19.2 %all-to-all-start = ((bf16[128,5,128]{2,1,0:T(8,128)(2,1)}), bf16[128,5,128]{2,1,0:T(8,128)(2,1)S(1)}, u32[]{:S(2)}, u32[]{:S(2)}) async-start(bf16[128,5,128]{2,1,0:T(8,128)(2,1)} %scatter_fusion.1), calls=%async_computation | async-start | bytes 524288 | tf_op jit(solution)/shard_map/all_to_all | solution.py:174
  38.7 0.3 all-reduce.4.cloned.1.call-start
  39.2 3.1 fusion.41
  42.3 3.2 fusion.40
  45.6 3.2 fusion.43
  48.8 3.2 fusion.42
  52.0 6.2 all-to-all-done
  58.5 0.2 broadcast_in_dim.65
  58.7 135.2 %while.13 = (s32[]{:T(128)}, f32[64,64,128]{2,1,0:T(8,128)S(1)}, s32[4,32,3]{1,0,2:T(4,128)S(1)}, bf16[4,32,4,128]{3,1,0,2:T(8,128)(2,1)S(1)}, s32[]{:T(128)}, /*index=5*/f32[64]{0:T(128)S(1)}, s32[]{:T(128)}) while((s32[]{:T(128)}, f32[64,64,128]{2,1,0:T(8,128)S(1)}, s32[4,32,3]{1,0,2:T(4,128)S(1)}, ...), condition=%wide.region_6.7_spmd.clone, body=%wide.region_4.6_spmd.clone.sunk | while | flops 151425568 | bytes 14077401 | solution.py:199
  59.3 15.9 %fusion.136 = (bf16[32,128,64]{2,1,0:T(8,128)(2,1)S(1)}, bf16[32,128,64]{2,1,0:T(8,128)(2,1)S(1)}, bf16[32,128,64]{2,1,0:T(8,128)(2,1)S(1)}, bf16[32,128,64]{2,1,0:T(8,128)(2,1)S(1)}) fusion(f32[32,128]{1,0:T(8,128)S(1)} %get-tuple-element.234, f32[32,128]{1,0:T(8,128)S(1)} %get-tuple-element.235, f32[32,128]{1,0:T(8,128)S(1)} %get-tuple-element.236, ...), kind=kLoop, calls=%fused_computation.14.clone.2 | loop fusion | flops 3145728 | bytes 2162944 | tf_op jit(solution)/shard_map/while/body/eval_jaxpr/convert_element_type | solution.py:43
  75.3 8.4 %fusion.137 = bf16[32,128,64]{2,1,0:T(8,128)(2,1)S(1)} fusion(f32[32,128]{1,0:T(8,128)S(1)} %get-tuple-element.234, f32[64]{0:T(128)S(1)} %add_multiply_fusion.9, f32[32,128]{1,0:T(8,128)S(1)} %get-tuple-element.235, f32[32,128]{1,0:T(8,128)S(1)} %get-tuple-element.236), kind=kLoop, calls=%fused_computation.56.clone.1 | loop fusion | flops 2097152 | bytes 573696 | tf_op jit(solution)/shard_map/while/body/eval_jaxpr/neg | solution.py:48
  83.7 2.4 fusion.138
  86.2 4.2 fusion.140
  90.5 0.3 pad_maximum_fusion.4
  90.8 2.1 scatter_fusion
  93.0 15.9 %fusion.136 = (bf16[32,128,64]{2,1,0:T(8,128)(2,1)S(1)}, bf16[32,128,64]{2,1,0:T(8,128)(2,1)S(1)}, bf16[32,128,64]{2,1,0:T(8,128)(2,1)S(1)}, bf16[32,128,64]{2,1,0:T(8,128)(2,1)S(1)}) fusion(f32[32,128]{1,0:T(8,128)S(1)} %get-tuple-element.234, f32[32,128]{1,0:T(8,128)S(1)} %get-tuple-element.235, f32[32,128]{1,0:T(8,128)S(1)} %get-tuple-element.236, ...), kind=kLoop, calls=%fused_computation.14.clone.2 | loop fusion | flops 3145728 | bytes 2162944 | tf_op jit(solution)/shard_map/while/body/eval_jaxpr/convert_element_type | solution.py:43
  108.9 8.4 %fusion.137 = bf16[32,128,64]{2,1,0:T(8,128)(2,1)S(1)} fusion(f32[32,128]{1,0:T(8,128)S(1)} %get-tuple-element.234, f32[64]{0:T(128)S(1)} %add_multiply_fusion.9, f32[32,128]{1,0:T(8,128)S(1)} %get-tuple-element.235, f32[32,128]{1,0:T(8,128)S(1)} %get-tuple-element.236), kind=kLoop, calls=%fused_computation.56.clone.1 | loop fusion | flops 2097152 | bytes 573696 | tf_op jit(solution)/shard_map/while/body/eval_jaxpr/neg | solution.py:48
  117.4 2.4 fusion.138
  119.9 4.2 fusion.140
  124.1 0.3 pad_maximum_fusion.4
  124.5 2.1 scatter_fusion
  126.7 15.9 %fusion.136 = (bf16[32,128,64]{2,1,0:T(8,128)(2,1)S(1)}, bf16[32,128,64]{2,1,0:T(8,128)(2,1)S(1)}, bf16[32,128,64]{2,1,0:T(8,128)(2,1)S(1)}, bf16[32,128,64]{2,1,0:T(8,128)(2,1)S(1)}) fusion(f32[32,128]{1,0:T(8,128)S(1)} %get-tuple-element.234, f32[32,128]{1,0:T(8,128)S(1)} %get-tuple-element.235, f32[32,128]{1,0:T(8,128)S(1)} %get-tuple-element.236, ...), kind=kLoop, calls=%fused_computation.14.clone.2 | loop fusion | flops 3145728 | bytes 2162944 | tf_op jit(solution)/shard_map/while/body/eval_jaxpr/convert_element_type | solution.py:43
  142.6 8.4 %fusion.137 = bf16[32,128,64]{2,1,0:T(8,128)(2,1)S(1)} fusion(f32[32,128]{1,0:T(8,128)S(1)} %get-tuple-element.234, f32[64]{0:T(128)S(1)} %add_multiply_fusion.9, f32[32,128]{1,0:T(8,128)S(1)} %get-tuple-element.235, f32[32,128]{1,0:T(8,128)S(1)} %get-tuple-element.236), kind=kLoop, calls=%fused_computation.56.clone.1 | loop fusion | flops 2097152 | bytes 573696 | tf_op jit(solution)/shard_map/while/body/eval_jaxpr/neg | solution.py:48
  151.0 2.4 fusion.138
  153.6 4.2 fusion.140
  157.8 0.3 pad_maximum_fusion.4
  158.2 2.1 scatter_fusion
  160.4 15.9 %fusion.136 = (bf16[32,128,64]{2,1,0:T(8,128)(2,1)S(1)}, bf16[32,128,64]{2,1,0:T(8,128)(2,1)S(1)}, bf16[32,128,64]{2,1,0:T(8,128)(2,1)S(1)}, bf16[32,128,64]{2,1,0:T(8,128)(2,1)S(1)}) fusion(f32[32,128]{1,0:T(8,128)S(1)} %get-tuple-element.234, f32[32,128]{1,0:T(8,128)S(1)} %get-tuple-element.235, f32[32,128]{1,0:T(8,128)S(1)} %get-tuple-element.236, ...), kind=kLoop, calls=%fused_computation.14.clone.2 | loop fusion | flops 3145728 | bytes 2162944 | tf_op jit(solution)/shard_map/while/body/eval_jaxpr/convert_element_type | solution.py:43
  176.3 8.4 %fusion.137 = bf16[32,128,64]{2,1,0:T(8,128)(2,1)S(1)} fusion(f32[32,128]{1,0:T(8,128)S(1)} %get-tuple-element.234, f32[64]{0:T(128)S(1)} %add_multiply_fusion.9, f32[32,128]{1,0:T(8,128)S(1)} %get-tuple-element.235, f32[32,128]{1,0:T(8,128)S(1)} %get-tuple-element.236), kind=kLoop, calls=%fused_computation.56.clone.1 | loop fusion | flops 2097152 | bytes 573696 | tf_op jit(solution)/shard_map/while/body/eval_jaxpr/neg | solution.py:48
  184.7 2.4 fusion.138
  187.3 4.2 fusion.140
  191.5 0.3 pad_maximum_fusion.4
  191.8 2.1 scatter_fusion
  194.0 1.5 reshape.508
  195.5 0.2 all-reduce.6.cloned.1.call-start
  195.8 0.4 copy-done.4
  196.3 0.3 copy-done.1
  196.5 2.4 fusion.38
  198.9 2.4 fusion.37
  201.3 2.4 fusion.36
  203.7 2.4 fusion.35
  206.1 64.2 %all-reduce.4.cloned.1.call-done = f32[2,32,8192]{2,1,0:T(8,128)} async-done(((f32[2,32,8192]{2,1,0:T(8,128)}), f32[2,32,8192]{2,1,0:T(8,128)}) %all-reduce.4.cloned.1.call-update) | async-done | bytes 2097168 | tf_op jit(solution)/shard_map/psum | solution.py:202
  270.2 1.1 copy_bitcast_fusion.1
  271.5 0.9 convolution_bitcast_fusion
  272.5 1.8 fusion.39
  274.3 0.2 slice_negate_fusion
  274.5 1.3 fusion.45
  276.0 1.1 convolution_add_fusion.1
  277.1 0.6 fusion.51
  277.7 0.6 fusion.49
  278.4 0.7 convolution_subtract_fusion
  279.1 0.7 convolution_add_fusion
  279.8 1.0 maximum_multiply_fusion
  280.9 459.1 %all-reduce.6.cloned.1.call-done = f32[1024,128]{1,0:T(8,128)} async-done(((f32[1024,128]{1,0:T(8,128)}), f32[1024,128]{1,0:T(8,128)}) %all-reduce.6.cloned.1.call-update) | async-done | bytes 524304
  740.0 1.2 constant_dynamic-slice_fusion.1
  (71 shorter events, 1.9 us)
Async XLA Ops:
  19.5 38.6 %all-to-all-start = ((bf16[128,5,128]{2,1,0:T(8,128)(2,1)}), bf16[128,5,128]{2,1,0:T(8,128)(2,1)S(1)}, u32[]{:S(2)}, u32[]{:S(2)}) async-start(bf16[128,5,128]{2,1,0:T(8,128)(2,1)} %scatter_fusion.1), calls=%async_computation | async-start | bytes 524288 | tf_op jit(solution)/shard_map/all_to_all | solution.py:174
  38.7 231.6 %all-reduce.4.cloned.1.call-start = ((), (), s32[]{:S(2)}) async-start(), calls=%async_computation.1 | async-start | bytes 4194304 | tf_op jit(solution)/shard_map/psum | solution.py:202
  195.5 0.7 copy-start.4
  195.5 1.1 copy-start.1
  195.5 3.4 copy-start
  195.5 5.8 copy-start.3
  195.5 8.2 %copy-start.2 = (f32[16,64,64]{2,1,0:T(8,128)S(1)}, f32[16,64,64]{2,1,0:T(8,128)}, u32[]{:S(2)}) copy-start(f32[16,64,64]{2,1,0:T(8,128)} %fusion.42) | copy-start | bytes 786436
  195.5 544.4 %all-reduce.6.cloned.1.call-start = ((), (), s32[]{:S(2)}) async-start(), calls=%async_computation.2 | async-start | bytes 1048576
Sparse Core Ops, SparseCore 0:
  195.6 74.5 all-reduce.3
  281.0 458.9 all-reduce.5
where the time goes:
time: 752 us; the launch traced here: 748 us
  waiting for transfers between devices  529 us (70%)
  other arithmetic  132 us (18%)
  matrix products  39.5 us (5%)
  starting transfers between devices  19.7 us (3%)
  between operations  14.6 us (2%)
  local copies, waits for them, and re-layouts  12.5 us (2%)
    unnamed x3, waiting for transfers between devices  459 us
    psum x1, waiting for transfers between devices, shards(): summed_towers = lax.psum(flat_towers, 'wa')  64.2 us
    convert_element_type x4, other arithmetic, phasor_tables(): (real_part * sine_v + imag_part * cosine_v).astype(jnp.bfloat16)  63.7 us
    neg x4, other arithmetic, phasor_tables(): lower_rows = jnp.concatenate([-weighted_imag, weighted_real], axis=2)  33.6 us
    all_to_all x1, starting transfers between devices, shards(): lax.all_to_all(outgoing, 'col', split_axis=0, concat_axis=0, tiled=True)  19.2 us
    sub x4, other arithmetic, complex_times(): operand_real * factor_real - operand_imag * factor_imag  16.9 us
  transfers between devices with their start and end apart: 3, of which 3 were waited for; matrix products, arithmetic and copies ran while one was open for 3% of the time, Pallas kernels for 0%

commit v1 on v0

v1 whole, which is shorter than its diff:
```python
import functools
import math

import jax
import jax.numpy as jnp
import numpy as np
from jax import lax
from jax.experimental import pallas as pl
from jax.experimental.pallas import tpu as pltpu
from jax.sharding import PartitionSpec as P

S = 64
BLOCK_VISIBILITY = 128
RANGE_PLANES = 16
FACETS = 16
TOUCH = 12
DEVICE_COLUMNS = 2
COLUMN_SUBGRIDS = 32
DEVICE_SLOTS = 64
N_COL = 64
N_WA = 8

FULL_TURN = 2.0 * math.pi
FIELD_WIDTH = 0.2
CELL_STEP = 0.37
WTERM_LIMIT = 4000.0
SCALE = 1.0 / math.sqrt(BLOCK_VISIBILITY * N_COL * N_WA * DEVICE_SLOTS)
UNROLL = 4

f32 = jnp.float32
bf16 = jnp.bfloat16


def half_turn_fits():
    nodes = np.cos(np.pi * (np.arange(400) + 0.5) / 400) * 0.125 + 0.125
    root = np.sqrt(nodes)
    sine = np.polynomial.chebyshev.Chebyshev.fit(nodes, np.sin(np.pi * root) / root, 4, domain=[0, 0.25])
    cosine = np.polynomial.chebyshev.Chebyshev.fit(nodes, np.cos(np.pi * root), 5, domain=[0, 0.25])
    return tuple(
        [float(c) for c in fit.convert(kind=np.polynomial.Polynomial).coef] for fit in (sine, cosine)
    )


SINE_FIT, COSINE_FIT = half_turn_fits()


def horner(fit, z):
    total = fit[-1]
    for c in fit[-2::-1]:
        total = total * z + c
    return total


def cos_sin_turns(turns):
    h = turns - jnp.floor(turns + 0.5)
    z = h * h
    sine = h * horner(SINE_FIT, z)
    cosine = horner(COSINE_FIT, z)
    return 1.0 - 2.0 * (sine * sine), 2.0 * (sine * cosine)


def grid_kernel(cells, first_plane, vis_ref, uv_ref, out_ref, vis_rows, uv_rows, screen_a, screen_b):
    vis_rows[...] = vis_ref[...].astype(f32)
    uv_rows[...] = uv_ref[...].astype(f32)

    lane = lax.broadcasted_iota(jnp.int32, (S, 2 * S), 1)
    a = (lax.broadcasted_iota(jnp.int32, (S, 2 * S), 0) - S // 2).astype(f32) * (FIELD_WIDTH / S)
    e = ((lane & (S - 1)) - S // 2).astype(f32) * (FIELD_WIDTH / S)
    radius = a * a + e * e
    lag = -radius / (1.0 + jnp.sqrt(1.0 - radius))
    sign = jnp.where(lane < S, -1.0, 1.0).astype(f32)
    plane_step = 2.0 * WTERM_LIMIT / (RANGE_PLANES * N_WA)

    def make_screen(p, carry):
        depth = -WTERM_LIMIT + ((first_plane[0] + p).astype(f32) + 0.5) * plane_step
        cosine, sine = cos_sin_turns(depth * lag)
        screen_a[p] = cosine
        screen_b[p] = sine * sign
        return carry

    lax.fori_loop(0, RANGE_PLANES, make_screen, 0)

    fine = lax.broadcasted_iota(jnp.int32, (8, 1), 0).astype(f32) * (1.0 / S)
    coarse = (lax.broadcasted_iota(jnp.int32, (8, 1), 0) - 4).astype(f32) * (8.0 / S)

    def one_block(b):
        u = uv_rows[pl.ds(2 * b, 1), :]
        v = uv_rows[pl.ds(2 * b + 1, 1), :]
        vr = vis_rows[pl.ds(2 * b, 1), :]
        vi = vis_rows[pl.ds(2 * b + 1, 1), :]
        turns = jnp.concatenate([u * fine, u * coarse, v * fine, v * coarse], axis=0)
        c, s = cos_sin_turns(turns)
        cu, su, cua, sua = c[0:8], s[0:8], c[8:16], s[8:16]
        cv, sv, cva, sva = c[16:24], s[16:24], c[24:32], s[24:32]
        wra = vr * cva - vi * sva
        wia = vr * sva + vi * cva
        uc, us, wr, wi = [], [], [], []
        for k in range(8):
            ck, sk = cua[k : k + 1], sua[k : k + 1]
            uc.append(ck * cu - sk * su)
            us.append(sk * cu + ck * su)
            rk, ik = wra[k : k + 1], wia[k : k + 1]
            wr.append(rk * cv - ik * sv)
            wi.append(rk * sv + ik * cv)
        uc, us, wr, wi = [jnp.concatenate(t, axis=0).astype(bf16) for t in (uc, us, wr, wi)]
        left = jnp.concatenate([uc, us], axis=1)
        right = jnp.concatenate(
            [jnp.concatenate([wr, -wi], axis=1), jnp.concatenate([wi, wr], axis=1)], axis=0
        )
        grid = lax.dot_general(
            left, right, (((1,), (1,)), ((), ())), preferred_element_type=f32
        )
        plane = cells[b] & (RANGE_PLANES - 1)
        towers = grid * screen_a[plane] + pltpu.roll(grid, S, 1) * screen_b[plane]
        out_ref[pl.ds(b, S, stride=DEVICE_SLOTS), :] = towers

    def some_blocks(i, carry):
        for k in range(UNROLL):
            one_block(i * UNROLL + k)
        return carry

    lax.fori_loop(0, DEVICE_SLOTS // UNROLL, some_blocks, 0)


def split_bf16(x):
    high = x.astype(bf16)
    return high, (x - high.astype(f32)).astype(bf16)


def facet_kernel(live, owner_ref, cell_ref, touch_ref, shift_ref, towers_ref, out_ref, facet_ref):
    cell = cell_ref[...]
    column = owner_ref[...] * DEVICE_COLUMNS + cell // (COLUMN_SUBGRIDS * RANGE_PLANES)
    row = (cell // RANGE_PLANES) % COLUMN_SUBGRIDS
    facet = lax.broadcasted_iota(jnp.int32, (FACETS, 1), 0)
    fx = (facet % 4).astype(f32)
    fy = (facet // 4).astype(f32)
    columns = DEVICE_COLUMNS * N_COL
    turns = CELL_STEP * (
        (column.astype(f32) - columns / 2 + 0.5) * ((fx - 1.5) / 4)
        + (row.astype(f32) - COLUMN_SUBGRIDS / 2 + 0.5) * ((fy - 1.5) / 4)
    )
    cosine, sine = cos_sin_turns(turns)
    named = touch_ref[...]
    facet_lane = lax.broadcasted_iota(jnp.int32, (columns, FACETS), 1)
    touched = named[:, 0:1] == facet_lane
    for t in range(1, TOUCH):
        touched = touched | (named[:, t : t + 1] == facet_lane)
    touched = jnp.where(touched, 1.0, 0.0).astype(bf16)
    chosen = lax.broadcasted_iota(jnp.int32, (columns, DEVICE_SLOTS), 0) == column
    alive = lax.broadcasted_iota(jnp.int32, (columns, DEVICE_SLOTS), 1) < live[0]
    chosen = jnp.where(chosen & alive, 1.0, 0.0).astype(bf16)
    mask = lax.dot_general(touched, chosen, (((0,), (0,)), ((), ())), preferred_element_type=f32)
    weights = jnp.concatenate([cosine * mask, sine * mask], axis=0)
    high, low = split_bf16(weights)
    left = jnp.concatenate(
        [jnp.concatenate([high, high], axis=1), jnp.concatenate([low, jnp.zeros_like(low)], axis=1)],
        axis=0,
    )
    sign = jnp.where(lax.broadcasted_iota(jnp.int32, (FACETS, 2 * S), 1) < S, -1.0, 1.0).astype(f32)

    for l in range(0, S, 2):
        pair = jnp.concatenate(
            [
                towers_ref[l * DEVICE_SLOTS : (l + 1) * DEVICE_SLOTS, :],
                towers_ref[(l + 1) * DEVICE_SLOTS : (l + 2) * DEVICE_SLOTS, :],
            ],
            axis=1,
        )
        high, low = split_bf16(pair)
        sums = jnp.dot(left, jnp.concatenate([high, low], axis=0), preferred_element_type=f32)
        sums = sums[: 2 * FACETS] + sums[2 * FACETS :]
        for k in range(2):
            part = sums[:, 2 * S * k : 2 * S * (k + 1)]
            facet_ref[pl.ds(l + k, FACETS, stride=S), :] = (
                part[:FACETS] + sign * pltpu.roll(part[FACETS:], S, 1)
            )

    wide = jnp.where(lax.broadcasted_iota(jnp.int32, (S, 2 * S), 1) < S, -1.0, 1.0).astype(f32)
    for fx in range(4):
        plain = [facet_ref[(fx + 4 * fy) * S : (fx + 4 * fy + 1) * S, :] for fy in range(4)]
        turned = [wide * pltpu.roll(g, S, 1) for g in plain]
        stack = jnp.concatenate(
            [jnp.concatenate(plain, axis=1), jnp.concatenate(turned, axis=1)], axis=0
        )
        high, low = split_bf16(stack)
        shift = shift_ref[fx]
        first = jnp.dot(shift, high, preferred_element_type=f32)
        second = jnp.dot(shift[:S], low, preferred_element_type=f32)
        image = (first[:S] + first[S:] + second).reshape(N_WA, S // N_WA, 8 * S)
        rows = jnp.concatenate(
            [image[:, :, 2 * S * fy : 2 * S * (fy + 1)] for fy in range(4)], axis=1
        )
        out_ref[:, fx * 32 : (fx + 1) * 32, :] = rows.astype(out_ref.dtype)


def shift_matrix(d):
    k = np.arange(S) - S // 2
    x = np.arange(S)
    return np.exp(2j * np.pi * k * x[:, None] / S) @ np.exp(-2j * np.pi * k[:, None] * (x + d) / S) / S


def left_shifts():
    order = np.array([16 * q + 2 * w + i for w in range(N_WA) for q in range(4) for i in range(2)])
    tables = []
    for fx in range(4):
        shift = shift_matrix((fx + 0.5) / 4)[order] * SCALE
        table = np.concatenate([shift.real, shift.imag], axis=1).astype(np.float32)
        high = table.astype(jnp.bfloat16)
        low = (table - high.astype(np.float32)).astype(jnp.bfloat16)
        tables.append(np.concatenate([high, low], axis=0))
    return np.stack(tables)


def right_shifts():
    tables = []
    for fy in range(4):
        shift = shift_matrix((fy + 0.5) / 4).T
        tables.append(
            np.concatenate(
                [
                    np.concatenate([shift.real, shift.imag], axis=1),
                    np.concatenate([-shift.imag, shift.real], axis=1),
                ],
                axis=0,
            )
        )
    return np.stack(tables).astype(np.float32)


def middle_kernel(in_ref, out_ref):
    total = in_ref[0].astype(f32)
    for k in range(1, N_WA):
        total = total + in_ref[k].astype(f32)
    for fy in range(4):
        for fx in range(4):
            out_ref[(4 * fy + fx) * 8 : (4 * fy + fx + 1) * 8, :] = total[
                fx * 32 + fy * 8 : fx * 32 + fy * 8 + 8
            ]


def last_kernel(facet_row, in_ref, shift_ref, out_ref):
    total = in_ref[0]
    for k in range(1, N_COL):
        total = total + in_ref[k]
    rows = jnp.concatenate([total, jnp.zeros((6, 2 * S), f32)], axis=0)
    image = jnp.dot(rows, shift_ref[facet_row[0]], precision=lax.Precision.HIGHEST, preferred_element_type=f32)
    out_ref[...] = image[:2]


VMEM = pl.BlockSpec(memory_space=pltpu.VMEM)
SMEM = pl.BlockSpec(memory_space=pltpu.SMEM)


def shards(
    visibilities,
    visibility_uv_offsets,
    block_owner_index,
    block_cell_number,
    live_counts,
    touch_lists,
):
    col_index = lax.axis_index("col")
    range_index = lax.axis_index("wa")
    named = lax.all_to_all(
        jnp.broadcast_to(touch_lists[None], (N_COL, DEVICE_COLUMNS, TOUCH)),
        "col",
        split_axis=0,
        concat_axis=0,
        tiled=True,
    ).reshape(N_COL * DEVICE_COLUMNS, TOUCH)
    cells = block_cell_number.reshape(DEVICE_SLOTS)
    towers = pl.pallas_call(
        grid_kernel,
        out_shape=jax.ShapeDtypeStruct((S * DEVICE_SLOTS, 2 * S), f32),
        in_specs=[SMEM, SMEM, VMEM, VMEM],
        out_specs=VMEM,
        scratch_shapes=[
            pltpu.VMEM((2 * DEVICE_SLOTS, BLOCK_VISIBILITY), f32),
            pltpu.VMEM((2 * DEVICE_SLOTS, BLOCK_VISIBILITY), f32),
            pltpu.VMEM((RANGE_PLANES, S, 2 * S), f32),
            pltpu.VMEM((RANGE_PLANES, S, 2 * S), f32),
        ],
        compiler_params=pltpu.CompilerParams(vmem_limit_bytes=24 * 1024 * 1024),
        cost_estimate=pl.CostEstimate(flops=300_000_000, bytes_accessed=2_200_000, transcendentals=0),
        name="grid_blocks",
    )(
        cells,
        (range_index * RANGE_PLANES).reshape(1).astype(jnp.int32),
        visibilities.reshape(2 * DEVICE_SLOTS, BLOCK_VISIBILITY),
        visibility_uv_offsets.reshape(2 * DEVICE_SLOTS, BLOCK_VISIBILITY),
    )
    partial_rows = pl.pallas_call(
        facet_kernel,
        out_shape=jax.ShapeDtypeStruct((N_WA, FACETS * S // N_WA, 2 * S), bf16),
        in_specs=[SMEM, VMEM, VMEM, VMEM, VMEM, VMEM],
        out_specs=VMEM,
        scratch_shapes=[pltpu.VMEM((FACETS * S, 2 * S), f32)],
        compiler_params=pltpu.CompilerParams(vmem_limit_bytes=24 * 1024 * 1024),
        name="facet_sums",
    )(
        live_counts.reshape(1),
        block_owner_index.reshape(1, DEVICE_SLOTS),
        block_cell_number.reshape(1, DEVICE_SLOTS),
        named,
        jnp.asarray(left_shifts()),
        towers,
    )
    arrived = lax.all_to_all(partial_rows, "wa", split_axis=0, concat_axis=0, tiled=True)
    range_rows = pl.pallas_call(
        middle_kernel,
        out_shape=jax.ShapeDtypeStruct((FACETS * S // N_WA, 2 * S), f32),
        in_specs=[VMEM],
        out_specs=VMEM,
        name="range_sums",
    )(arrived)
    arrived = lax.all_to_all(
        range_rows.reshape(N_COL, 2, 2 * S), "col", split_axis=0, concat_axis=0, tiled=True
    )
    return pl.pallas_call(
        last_kernel,
        out_shape=jax.ShapeDtypeStruct((2, 2 * S), f32),
        in_specs=[SMEM, VMEM, VMEM],
        out_specs=VMEM,
        name="column_sums",
    )((col_index // 16).reshape(1).astype(jnp.int32), arrived, jnp.asarray(right_shifts()))


def solution(mesh):
    placed = (
        P("col", "wa", None, None, None),
        P("col", "wa", None, None, None),
        P("col", "wa", None, None),
        P("col", "wa", None),
        P("col", "wa"),
        P("col", None),
    )
    return jax.shard_map(
        shards, mesh=mesh, in_specs=placed, out_specs=P(("col", "wa"), None), check_vma=False
    )
```

time: 752 us -> 77.6 us (0.10)
  waiting for transfers between devices: 529 us -> 17.9 us
  other arithmetic: 132 us -> 0 us
  matrix products: 39.5 us -> 0 us
  between operations: 14.6 us -> 0.72 us
  blocking collectives: 0 us -> 13 us
  Pallas kernels: 0 us -> 12.4 us
  starting transfers between devices: 19.7 us -> 28.9 us
  local copies, waits for them, and re-layouts: 12.5 us -> 4.16 us
    unnamed x3 -> x0, waiting for transfers between devices: 459 us -> none
    convert_element_type x13 -> x0, other arithmetic: 64.8 us -> none  [the longest x4 63.7 us: phasor_tables(): (real_part * sine_v + imag_part * cosine_v).astype(jnp.bfloat16)]
    psum x1 -> x0, waiting for transfers between devices: 64.2 us -> none  [shards(): summed_towers = lax.psum(flat_towers, 'wa')]
    dot_general x20 -> x0, matrix products: 39.5 us -> none  [the longest x4 9.6 us: grid_tile(): jnp.einsum('nkl,nkq->nlq', left_table, right_table, preferred_element_typ...]
    neg x6 -> x0, other arithmetic: 34 us -> none  [the longest x4 33.6 us: phasor_tables(): lower_rows = jnp.concatenate([-weighted_imag, weighted_real], axis=2)]
    sub x4 -> x0, other arithmetic: 16.9 us -> none  [complex_times(): operand_real * factor_real - operand_imag * factor_imag]
    all_to_all x0 -> x1, blocking collectives: none -> 13 us  [shards(): lax.all_to_all(partial_rows, 'wa', split_axis=0, concat_axis=0, tiled=True)]
    pallas_call x0 -> x4, Pallas kernels: none -> 12.4 us  [the longest x1 7.34 us: shards(): pl.pallas_call(grid_kernel, out_shape=jax.ShapeDtypeStruct((S * DEVICE_SL...]
  transfers between devices with their start and end apart: 3 -> 2, of which waited for: 3 -> 2; matrix products, arithmetic and copies ran while one was open for 3% -> 0% of each run, Pallas kernels for 0% -> 10%
where the time goes in v1:
time: 77.6 us; the launch traced here: 77.2 us
  starting transfers between devices  28.9 us (37%)
  waiting for transfers between devices  17.9 us (23%)
  blocking collectives  13 us (17%)
  Pallas kernels  12.4 us (16%)
  local copies, waits for them, and re-layouts  4.16 us (5%)
    all_to_all x1, starting transfers between devices, shards(): lax.all_to_all(jnp.broadcast_to(touch_lists[None], (N_COL, DEVICE_COLUMNS...  19.1 us
    all_to_all x1, waiting for transfers between devices, shards(): lax.all_to_all(range_rows.reshape(N_COL, 2, 2 * S), 'col', split_axis=0,...  14.1 us
    all_to_all x1, blocking collectives, shards(): lax.all_to_all(partial_rows, 'wa', split_axis=0, concat_axis=0, tiled=True)  13 us
    all_to_all x1, starting transfers between devices, shards(): lax.all_to_all(range_rows.reshape(N_COL, 2, 2 * S), 'col', split_axis=0,...  9.82 us
    pallas_call x1, Pallas kernels, shards(): pl.pallas_call(grid_kernel, out_shape=jax.ShapeDtypeStruct((S * DEVICE_SL...  7.34 us
    all_to_all x1, waiting for transfers between devices, shards(): lax.all_to_all(jnp.broadcast_to(touch_lists[None], (N_COL, DEVICE_COLUMNS...  3.83 us
    unnamed x14, local copies, waits for them, and re-layouts  2.8 us
    pallas_call x1, Pallas kernels, shards(): pl.pallas_call(last_kernel, out_shape=jax.ShapeDtypeStruct((2, 2 * S), f3...  1.77 us
  transfers between devices with their start and end apart: 2, of which 2 were waited for; matrix products, arithmetic and copies ran while one was open for 0% of the time, Pallas kernels for 10%

profile of v1, /device:TPU:1, one launch (start us, length us, event | category | flops | bytes accessed | tf_op | source)
XLA Modules:
  0.0 77.2 jit_solution(1402484880741155527)
XLA Ops:
  0.0 0.0 copy-start
  0.0 0.0 copy-start.4
  0.0 0.0 copy-start.5
  0.0 1.4 %broadcast_in_dim.2 = s32[64,2,12]{2,1,0:T(2,128)} broadcast(s32[2,12]{1,0:T(2,128)} %param.13), dimensions={1,2} | broadcast | bytes 6240 | tf_op jit(solution)/shard_map/broadcast_in_dim | solution.py:265
  1.4 19.1 %all-to-all-start = ((s32[64,2,12]{2,1,0:T(2,128)}), s32[64,2,12]{2,1,0:T(2,128)S(1)}, u32[]{:S(2)}, u32[]{:S(2)}) async-start(s32[64,2,12]{2,1,0:T(2,128)} %broadcast_in_dim.2), calls=%async_computation | async-start | bytes 131072 | tf_op jit(solution)/shard_map/all_to_all | solution.py:264
  21.1 0.0 copy-start.1
  21.2 0.7 copy-done.1
  21.9 0.0 copy-start.2
  21.9 0.8 copy-done.2
  22.7 0.0 copy-start.3
  22.7 0.7 copy-done.3
  23.3 7.3 %grid_blocks.1.towers_ref = f32[4096,128]{1,0:T(8,128)S(1)} custom-call(s32[64]{0:T(128)S(1)} %bitcast.14, s32[1]{0:T(128)} %bitcast.6.first_plane, bf16[128,128]{1,0:T(8,128)(2,1)S(1)} %bitcast.12, bf16[128,128]{1,0:T(8,128)(2,1)S(1)} %bitcast.13), custom_call_target="tpu_custom_call" | custom-call | flops 300000000 | bytes 2200000 | tf_op jit(solution)/shard_map/grid_blocks/pallas_call | solution.py:272
  30.7 3.8 %all-to-all-done = s32[64,2,12]{2,1,0:T(2,128)S(1)} async-done(((s32[64,2,12]{2,1,0:T(2,128)}), s32[64,2,12]{2,1,0:T(2,128)S(1)}, u32[]{:S(2)}, u32[]{:S(2)}) %all-to-all-start) | async-done | bytes 6176 | tf_op jit(solution)/shard_map/all_to_all | solution.py:264
  34.5 0.0 copy-done
  34.5 0.0 copy-done.4
  34.5 0.0 copy-done.5
  34.5 1.7 %facet_sums.1 = bf16[8,128,128]{2,1,0:T(8,128)(2,1)S(1)} custom-call(s32[1]{0:T(128)} %bitcast.10.live, s32[1,64]{1,0:T(1,128)S(1)} %bitcast.16, s32[1,64]{1,0:T(1,128)S(1)} %bitcast.15, s32[128,12]{1,0:T(8,128)S(1)} %bitcast.11, bf16[4,128,128]{2,1,0:T(8,128)(2,1)S(1)} %copy-done, f32[4096,128]{1,0:T(8,128)S(1)} %grid_blocks.1.towers_ref), custom_call_target="tpu_custom_call" | custom-call | tf_op jit(solution)/shard_map/facet_sums/pallas_call | solution.py:292
  36.2 13.0 %all_to_all.15.in_ref = bf16[8,128,128]{2,1,0:T(8,128)(2,1)} all-to-all(bf16[8,128,128]{2,1,0:T(8,128)(2,1)S(1)} %facet_sums.1), channel_id=1, replica_groups=mesh['col'=64,'wa'=8] {'wa'}, dimensions={0} | all-to-all | bytes 524288 | tf_op jit(solution)/shard_map/all_to_all | solution.py:308
  49.2 1.6 %range_sums.1 = f32[128,128]{1,0:T(8,128)} custom-call(bf16[8,128,128]{2,1,0:T(8,128)(2,1)} %all_to_all.15.in_ref), custom_call_target="tpu_custom_call" | custom-call | tf_op jit(solution)/shard_map/range_sums/pallas_call | solution.py:309
  50.8 9.8 %all-to-all-start.2 = ((f32[64,2,128]{2,1,0:T(2,128)}), f32[64,2,128]{2,1,0:T(2,128)S(1)}, u32[]{:S(2)}, u32[]{:S(2)}) async-start(f32[64,2,128]{2,1,0:T(2,128)} %bitcast.17), calls=%async_computation.2 | async-start | bytes 131072 | tf_op jit(solution)/shard_map/all_to_all | solution.py:316
  60.7 14.1 %all-to-all-done.2.in_ref = f32[64,2,128]{2,1,0:T(2,128)S(1)} async-done(((f32[64,2,128]{2,1,0:T(2,128)}), f32[64,2,128]{2,1,0:T(2,128)S(1)}, u32[]{:S(2)}, u32[]{:S(2)}) %all-to-all-start.2) | async-done | bytes 65568 | tf_op jit(solution)/shard_map/all_to_all | solution.py:316
  74.8 0.0 copy-start.6
  74.8 0.6 copy-done.6
  75.4 1.8 %column_sums.1 = f32[2,128]{1,0:T(2,128)} custom-call(s32[1]{0:T(128)} %bitcast.facet_row, f32[64,2,128]{2,1,0:T(2,128)} %copy-done.6, f32[4,128,128]{2,1,0:T(8,128)} %constant.31.clone.shift_ref), custom_call_target="tpu_custom_call" | custom-call | tf_op jit(solution)/shard_map/column_sums/pallas_call | solution.py:319
Async XLA Ops:
  0.0 34.5 %copy-start = (bf16[4,128,128]{2,1,0:T(8,128)(2,1)S(1)}, bf16[4,128,128]{2,1,0:T(8,128)(2,1)}, u32[]{:S(2)}) copy-start(bf16[4,128,128]{2,1,0:T(8,128)(2,1)} %constant.30.clone.shift_ref) | copy-start | bytes 393220
  0.0 34.5 %copy-start.4 = (s32[1,1,64]{2,1,0:T(1,128)S(1)}, s32[1,1,64]{2,1,0:T(1,128)}, u32[]{:S(2)}) copy-start(s32[1,1,64]{2,1,0:T(1,128)} %param.11) | copy-start | bytes 772
  0.0 34.5 %copy-start.5 = (s32[1,1,64,1]{2,3,1,0:T(1,128)S(1)}, s32[1,1,64,1]{2,3,1,0:T(1,128)}, u32[]{:S(2)}) copy-start(s32[1,1,64,1]{2,3,1,0:T(1,128)} %param.10) | copy-start | bytes 772
  1.4 33.1 %all-to-all-start = ((s32[64,2,12]{2,1,0:T(2,128)}), s32[64,2,12]{2,1,0:T(2,128)S(1)}, u32[]{:S(2)}, u32[]{:S(2)}) async-start(s32[64,2,12]{2,1,0:T(2,128)} %broadcast_in_dim.2), calls=%async_computation | async-start | bytes 131072 | tf_op jit(solution)/shard_map/all_to_all | solution.py:264
  21.1 0.8 copy-start.1
  21.9 0.8 copy-start.2
  22.7 0.7 copy-start.3
  50.8 23.9 %all-to-all-start.2 = ((f32[64,2,128]{2,1,0:T(2,128)}), f32[64,2,128]{2,1,0:T(2,128)S(1)}, u32[]{:S(2)}, u32[]{:S(2)}) async-start(f32[64,2,128]{2,1,0:T(2,128)} %bitcast.17), calls=%async_computation.2 | async-start | bytes 131072 | tf_op jit(solution)/shard_map/all_to_all | solution.py:316
  74.8 0.6 copy-start.6

commit v2 on v1

--- a/solution.py
+++ b/solution.py
@@ -7,7 +7,7 @@
 from jax import lax
 from jax.experimental import pallas as pl
 from jax.experimental.pallas import tpu as pltpu
-from jax.sharding import PartitionSpec as P
+from jax.sharding import Mesh, PartitionSpec as P
 
 S = 64
 BLOCK_VISIBILITY = 128
@@ -26,6 +26,10 @@
 WTERM_LIMIT = 4000.0
 SCALE = 1.0 / math.sqrt(BLOCK_VISIBILITY * N_COL * N_WA * DEVICE_SLOTS)
 UNROLL = 4
+GROUP = 32
+TOUCH_Z, TOUCH_X = 10, 2
+PLANE_X, PLANE_WA = 0, 0
+LINE_Z = 8
 
 f32 = jnp.float32
 bf16 = jnp.bfloat16
@@ -59,9 +63,23 @@
     return 1.0 - 2.0 * (sine * sine), 2.0 * (sine * cosine)
 
 
-def grid_kernel(cells, first_plane, vis_ref, uv_ref, out_ref, vis_rows, uv_rows, screen_a, screen_b):
-    vis_rows[...] = vis_ref[...].astype(f32)
-    uv_rows[...] = uv_ref[...].astype(f32)
+def grid_kernel(
+    first_plane,
+    packed_ref,
+    out_ref,
+    cell_row,
+    cells,
+    vis_rows,
+    uv_rows,
+    screen_a,
+    screen_b,
+    arrival,
+):
+    cell_row[...] = packed_ref[4 * DEVICE_SLOTS : 4 * DEVICE_SLOTS + 8, :].astype(jnp.int32)
+    copy = pltpu.make_async_copy(cell_row, cells, arrival)
+    copy.start()
+    vis_rows[...] = packed_ref[: 2 * DEVICE_SLOTS, :]
+    uv_rows[...] = packed_ref[2 * DEVICE_SLOTS : 4 * DEVICE_SLOTS, :]
 
     lane = lax.broadcasted_iota(jnp.int32, (S, 2 * S), 1)
     a = (lax.broadcasted_iota(jnp.int32, (S, 2 * S), 0) - S // 2).astype(f32) * (FIELD_WIDTH / S)
@@ -79,6 +97,8 @@
         return carry
 
     lax.fori_loop(0, RANGE_PLANES, make_screen, 0)
+
+    copy.wait()
 
     fine = lax.broadcasted_iota(jnp.int32, (8, 1), 0).astype(f32) * (1.0 / S)
     coarse = (lax.broadcasted_iota(jnp.int32, (8, 1), 0) - 4).astype(f32) * (8.0 / S)
@@ -110,7 +130,7 @@
         grid = lax.dot_general(
             left, right, (((1,), (1,)), ((), ())), preferred_element_type=f32
         )
-        plane = cells[b] & (RANGE_PLANES - 1)
+        plane = cells[0, b] & (RANGE_PLANES - 1)
         towers = grid * screen_a[plane] + pltpu.roll(grid, S, 1) * screen_b[plane]
         out_ref[pl.ds(b, S, stride=DEVICE_SLOTS), :] = towers
 
@@ -127,7 +147,7 @@
     return high, (x - high.astype(f32)).astype(bf16)
 
 
-def facet_kernel(live, owner_ref, cell_ref, touch_ref, shift_ref, towers_ref, out_ref, facet_ref):
+def facet_kernel(live, owner_ref, cell_ref, touch_ref, shift_ref, towers_ref, out_ref, facet_ref, rows_ref):
     cell = cell_ref[...]
     column = owner_ref[...] * DEVICE_COLUMNS + cell // (COLUMN_SUBGRIDS * RANGE_PLANES)
     row = (cell // RANGE_PLANES) % COLUMN_SUBGRIDS
@@ -146,7 +166,10 @@
     for t in range(1, TOUCH):
         touched = touched | (named[:, t : t + 1] == facet_lane)
     touched = jnp.where(touched, 1.0, 0.0).astype(bf16)
-    chosen = lax.broadcasted_iota(jnp.int32, (columns, DEVICE_SLOTS), 0) == column
+    owner = owner_ref[...]
+    place = ((owner // 4 + 16 - TOUCH_Z) % 16) * 4 + (owner + 4 - TOUCH_X) % 4
+    place = place * DEVICE_COLUMNS + cell // (COLUMN_SUBGRIDS * RANGE_PLANES)
+    chosen = lax.broadcasted_iota(jnp.int32, (columns, DEVICE_SLOTS), 0) == place
     alive = lax.broadcasted_iota(jnp.int32, (columns, DEVICE_SLOTS), 1) < live[0]
     chosen = jnp.where(chosen & alive, 1.0, 0.0).astype(bf16)
     mask = lax.dot_general(touched, chosen, (((0,), (0,)), ((), ())), preferred_element_type=f32)
@@ -186,11 +209,14 @@
         shift = shift_ref[fx]
         first = jnp.dot(shift, high, preferred_element_type=f32)
         second = jnp.dot(shift[:S], low, preferred_element_type=f32)
-        image = (first[:S] + first[S:] + second).reshape(N_WA, S // N_WA, 8 * S)
-        rows = jnp.concatenate(
-            [image[:, :, 2 * S * fy : 2 * S * (fy + 1)] for fy in range(4)], axis=1
-        )
-        out_ref[:, fx * 32 : (fx + 1) * 32, :] = rows.astype(out_ref.dtype)
+        image = first[:S] + first[S:] + second
+        for fy in range(4):
+            place = (fx + 4 * fy - LINE_Z) % FACETS
+            for i in range(2):
+                rows_ref[pl.ds(2 * place + i, GROUP, stride=GROUP), :] = image[
+                    GROUP * i : GROUP * (i + 1), 2 * S * fy : 2 * S * (fy + 1)
+                ]
+    out_ref[...] = rows_ref[...].astype(bf16).reshape(GROUP, GROUP, 2 * S)
 
 
 def shift_matrix(d):
@@ -199,8 +225,18 @@
     return np.exp(2j * np.pi * k * x[:, None] / S) @ np.exp(-2j * np.pi * k[:, None] * (x + d) / S) / S
 
 
+def plane_group():
+    return [
+        ((x + PLANE_X) % 4) * N_WA + (wa + PLANE_WA) % N_WA for x in range(4) for wa in range(N_WA)
+    ]
+
+
+def line_group():
+    return [(z + LINE_Z) % FACETS for z in range(FACETS)]
+
+
 def left_shifts():
-    order = np.array([16 * q + 2 * w + i for w in range(N_WA) for q in range(4) for i in range(2)])
+    order = np.array([2 * dest + i for i in range(2) for dest in plane_group()])
     tables = []
     for fx in range(4):
         shift = shift_matrix((fx + 0.5) / 4)[order] * SCALE
@@ -224,27 +260,22 @@
                 axis=0,
             )
         )
-    return np.stack(tables).astype(np.float32)
-
-
-def middle_kernel(in_ref, out_ref):
+    table = np.stack(tables).astype(np.float32)
+    high = table.astype(jnp.bfloat16)
+    return np.concatenate([high, (table - high.astype(np.float32)).astype(jnp.bfloat16)], axis=2)
+
+
+def middle_kernel(in_ref, shift_ref, out_ref):
     total = in_ref[0].astype(f32)
-    for k in range(1, N_WA):
+    for k in range(1, GROUP):
         total = total + in_ref[k].astype(f32)
     for fy in range(4):
-        for fx in range(4):
-            out_ref[(4 * fy + fx) * 8 : (4 * fy + fx + 1) * 8, :] = total[
-                fx * 32 + fy * 8 : fx * 32 + fy * 8 + 8
-            ]
-
-
-def last_kernel(facet_row, in_ref, shift_ref, out_ref):
-    total = in_ref[0]
-    for k in range(1, N_COL):
-        total = total + in_ref[k]
-    rows = jnp.concatenate([total, jnp.zeros((6, 2 * S), f32)], axis=0)
-    image = jnp.dot(rows, shift_ref[facet_row[0]], precision=lax.Precision.HIGHEST, preferred_element_type=f32)
-    out_ref[...] = image[:2]
+        high, low = split_bf16(total[8 * fy : 8 * (fy + 1)])
+        both = jnp.concatenate([high, low], axis=0)
+        products = jnp.dot(both, shift_ref[(fy + LINE_Z // 4) % 4], preferred_element_type=f32)
+        out_ref[8 * fy : 8 * (fy + 1), :] = (
+            products[:8, : 2 * S] + products[:8, 2 * S :] + products[8:, : 2 * S]
+        )
 
 
 VMEM = pl.BlockSpec(memory_space=pltpu.VMEM)
@@ -259,81 +290,107 @@
     live_counts,
     touch_lists,
 ):
-    col_index = lax.axis_index("col")
     range_index = lax.axis_index("wa")
+    touch_group = [((z + TOUCH_Z) % 16) * 4 + (x + TOUCH_X) % 4 for z in range(16) for x in range(4)]
     named = lax.all_to_all(
         jnp.broadcast_to(touch_lists[None], (N_COL, DEVICE_COLUMNS, TOUCH)),
-        "col",
+        ("z", "x"),
         split_axis=0,
         concat_axis=0,
+        axis_index_groups=[touch_group],
         tiled=True,
     ).reshape(N_COL * DEVICE_COLUMNS, TOUCH)
-    cells = block_cell_number.reshape(DEVICE_SLOTS)
+    cells = block_cell_number.reshape(1, DEVICE_SLOTS)
+    shape = 4 * DEVICE_SLOTS + 8
+    half = 2 * DEVICE_SLOTS
+    packed = (
+        jnp.pad(visibilities.reshape(half, BLOCK_VISIBILITY), ((0, shape - half), (0, 0))).astype(f32)
+        + jnp.pad(
+            visibility_uv_offsets.reshape(half, BLOCK_VISIBILITY), ((half, 8), (0, 0))
+        ).astype(f32)
+        + jnp.pad(
+            cells, ((2 * half, 7), (0, BLOCK_VISIBILITY - DEVICE_SLOTS))
+        ).astype(f32)
+    )
     towers = pl.pallas_call(
         grid_kernel,
         out_shape=jax.ShapeDtypeStruct((S * DEVICE_SLOTS, 2 * S), f32),
-        in_specs=[SMEM, SMEM, VMEM, VMEM],
+        in_specs=[SMEM, VMEM],
         out_specs=VMEM,
         scratch_shapes=[
+            pltpu.VMEM((8, BLOCK_VISIBILITY), jnp.int32),
+            pltpu.SMEM((8, BLOCK_VISIBILITY), jnp.int32),
             pltpu.VMEM((2 * DEVICE_SLOTS, BLOCK_VISIBILITY), f32),
             pltpu.VMEM((2 * DEVICE_SLOTS, BLOCK_VISIBILITY), f32),
             pltpu.VMEM((RANGE_PLANES, S, 2 * S), f32),
             pltpu.VMEM((RANGE_PLANES, S, 2 * S), f32),
+            pltpu.SemaphoreType.DMA,
         ],
-        compiler_params=pltpu.CompilerParams(vmem_limit_bytes=24 * 1024 * 1024),
-        cost_estimate=pl.CostEstimate(flops=300_000_000, bytes_accessed=2_200_000, transcendentals=0),
+        compiler_params=pltpu.CompilerParams(vmem_limit_bytes=48 * 1024 * 1024),
+        cost_estimate=pl.CostEstimate(
+            flops=300_000_000, bytes_accessed=2_200_000, transcendentals=0
+        ),
         name="grid_blocks",
     )(
-        cells,
         (range_index * RANGE_PLANES).reshape(1).astype(jnp.int32),
-        visibilities.reshape(2 * DEVICE_SLOTS, BLOCK_VISIBILITY),
-        visibility_uv_offsets.reshape(2 * DEVICE_SLOTS, BLOCK_VISIBILITY),
+        packed,
     )
     partial_rows = pl.pallas_call(
         facet_kernel,
-        out_shape=jax.ShapeDtypeStruct((N_WA, FACETS * S // N_WA, 2 * S), bf16),
+        out_shape=jax.ShapeDtypeStruct((GROUP, GROUP, 2 * S), bf16),
         in_specs=[SMEM, VMEM, VMEM, VMEM, VMEM, VMEM],
         out_specs=VMEM,
-        scratch_shapes=[pltpu.VMEM((FACETS * S, 2 * S), f32)],
+        scratch_shapes=[
+            pltpu.VMEM((FACETS * S, 2 * S), f32),
+            pltpu.VMEM((FACETS * S, 2 * S), f32),
+        ],
         compiler_params=pltpu.CompilerParams(vmem_limit_bytes=24 * 1024 * 1024),
         name="facet_sums",
     )(
         live_counts.reshape(1),
         block_owner_index.reshape(1, DEVICE_SLOTS),
-        block_cell_number.reshape(1, DEVICE_SLOTS),
+        cells,
         named,
         jnp.asarray(left_shifts()),
         towers,
     )
-    arrived = lax.all_to_all(partial_rows, "wa", split_axis=0, concat_axis=0, tiled=True)
-    range_rows = pl.pallas_call(
+    arrived = lax.all_to_all(
+        partial_rows,
+        ("x", "wa"),
+        split_axis=0,
+        concat_axis=0,
+        axis_index_groups=[plane_group()],
+        tiled=True,
+    )
+    plane_rows = pl.pallas_call(
         middle_kernel,
-        out_shape=jax.ShapeDtypeStruct((FACETS * S // N_WA, 2 * S), f32),
-        in_specs=[VMEM],
+        out_shape=jax.ShapeDtypeStruct((GROUP, 2 * S), f32),
+        in_specs=[VMEM, VMEM],
         out_specs=VMEM,
-        name="range_sums",
-    )(arrived)
+        name="plane_sums",
+    )(arrived, jnp.asarray(right_shifts()))
     arrived = lax.all_to_all(
-        range_rows.reshape(N_COL, 2, 2 * S), "col", split_axis=0, concat_axis=0, tiled=True
-    )
-    return pl.pallas_call(
-        last_kernel,
-        out_shape=jax.ShapeDtypeStruct((2, 2 * S), f32),
-        in_specs=[SMEM, VMEM, VMEM],
-        out_specs=VMEM,
-        name="column_sums",
-    )((col_index // 16).reshape(1).astype(jnp.int32), arrived, jnp.asarray(right_shifts()))
+        plane_rows.reshape(FACETS, 2, 2 * S),
+        "z",
+        split_axis=0,
+        concat_axis=0,
+        axis_index_groups=[line_group()],
+        tiled=True,
+    )
+    return jnp.sum(arrived, axis=0)
 
 
 def solution(mesh):
+    grid = Mesh(mesh.devices.reshape(16, 4, N_WA), ("z", "x", "wa"))
+    col = ("z", "x")
     placed = (
-        P("col", "wa", None, None, None),
-        P("col", "wa", None, None, None),
-        P("col", "wa", None, None),
-        P("col", "wa", None),
-        P("col", "wa"),
-        P("col", None),
+        P(col, "wa", None, None, None),
+        P(col, "wa", None, None, None),
+        P(col, "wa", None, None),
+        P(col, "wa", None),
+        P(col, "wa"),
+        P(col, None),
     )
     return jax.shard_map(
-        shards, mesh=mesh, in_specs=placed, out_specs=P(("col", "wa"), None), check_vma=False
-    )
+        shards, mesh=grid, in_specs=placed, out_specs=P(("z", "x", "wa"), None), check_vma=False
+    )

time: 77.6 us -> 63.6 us (0.82)
  waiting for transfers between devices: 17.9 us -> 0.01 us
  blocking collectives: 13 us -> 28.3 us
  starting transfers between devices: 28.9 us -> 21 us
  local copies, waits for them, and re-layouts: 4.16 us -> 1.36 us
  Pallas kernels: 12.4 us -> 10.5 us
  other arithmetic: 0 us -> 1.39 us
    all_to_all x1 -> x2, blocking collectives: 13 us -> 28.3 us  [the longest x1 14.8 us: shards(): lax.all_to_all(partial_rows, ('x', 'wa'), split_axis=0, concat_axis=0, ax...]
    all_to_all x1 -> x0, waiting for transfers between devices: 14.1 us -> none  [shards(): lax.all_to_all(range_rows.reshape(N_COL, 2, 2 * S), 'col', split_axis=0,...]
    all_to_all x1 -> x0, starting transfers between devices: 9.82 us -> none  [shards(): lax.all_to_all(range_rows.reshape(N_COL, 2, 2 * S), 'col', split_axis=0,...]
    all_to_all x1, waiting for transfers between devices: 3.83 us -> 0.01 us  [shards(): lax.all_to_all(jnp.broadcast_to(touch_lists[None], (N_COL, DEVICE_COLUMNS...]
    unnamed x14 -> x6, local copies, waits for them, and re-layouts: 2.8 us -> 0.01 us
    all_to_all x1, starting transfers between devices: 19.1 us -> 21 us  [shards(): lax.all_to_all(jnp.broadcast_to(touch_lists[None], (N_COL, DEVICE_COLUMNS...]
    pallas_call x3 -> x2, Pallas kernels: 5.06 us -> 3.68 us  [the longest x1 1.87 us: shards(): pl.pallas_call(facet_kernel, out_shape=jax.ShapeDtypeStruct((GROUP, GROUP...]
    add x0 -> x1, other arithmetic: none -> 0.8 us  [shards(): jnp.pad(visibilities.reshape(half, BLOCK_VISIBILITY), ((0, shape - half),...]
  transfers between devices with their start and end apart: 2 -> 1, of which waited for: 2 -> 0; matrix products, arithmetic and copies ran while one was open for 0% -> 1% of each run, Pallas kernels for 10% -> 11%
where the time goes in v2:
time: 63.6 us; the launch traced here: 63.3 us
  blocking collectives  28.3 us (44%)
  starting transfers between devices  21 us (33%)
  Pallas kernels  10.5 us (17%)
  other arithmetic  1.39 us (2%)
  local copies, waits for them, and re-layouts  1.36 us (2%)
  between operations  0.72 us (1%)
    all_to_all x1, starting transfers between devices, shards(): lax.all_to_all(jnp.broadcast_to(touch_lists[None], (N_COL, DEVICE_COLUMNS...  21 us
    all_to_all x1, blocking collectives, shards(): lax.all_to_all(partial_rows, ('x', 'wa'), split_axis=0, concat_axis=0, ax...  14.8 us
    all_to_all x1, blocking collectives, shards(): lax.all_to_all(plane_rows.reshape(FACETS, 2, 2 * S), 'z', split_axis=0, c...  13.6 us
    pallas_call x1, Pallas kernels, shards(): pl.pallas_call(grid_kernel, out_shape=jax.ShapeDtypeStruct((S * DEVICE_SL...  6.82 us
    pallas_call x1, Pallas kernels, shards(): pl.pallas_call(facet_kernel, out_shape=jax.ShapeDtypeStruct((GROUP, GROUP...  1.87 us
    pallas_call x1, Pallas kernels, shards(): pl.pallas_call(middle_kernel, out_shape=jax.ShapeDtypeStruct((GROUP, 2 *...  1.81 us
    broadcast_in_dim x1, local copies, waits for them, and re-layouts, shards(): jnp.broadcast_to(touch_lists[None], (N_COL, DEVICE_COLUMNS, TOUCH))  1.34 us
  transfers between devices with their start and end apart: 1, of which 0 were waited for; matrix products, arithmetic and copies ran while one was open for 1% of the time, Pallas kernels for 11%

profile of v2, /device:TPU:1, one launch (start us, length us, event | category | flops | bytes accessed | tf_op | source)
XLA Modules:
  0.0 63.3 jit_solution(16380473050701362278)
XLA Ops:
  0.0 0.0 copy-start
  0.0 0.0 copy-start.1
  0.0 0.0 copy-start.2
  0.0 1.3 %broadcast_in_dim.2 = s32[64,2,12]{2,1,0:T(2,128)} broadcast(s32[2,12]{1,0:T(2,128)} %param.13), dimensions={1,2} | broadcast | bytes 6240 | tf_op jit(solution)/shard_map/broadcast_in_dim | solution.py:296
  1.4 21.0 %all-to-all-start = ((s32[64,2,12]{2,1,0:T(2,128)}), s32[64,2,12]{2,1,0:T(2,128)S(1)}, u32[]{:S(2)}, u32[]{:S(2)}) async-start(s32[64,2,12]{2,1,0:T(2,128)} %broadcast_in_dim.2), calls=%async_computation | async-start | bytes 131072 | tf_op jit(solution)/shard_map/all_to_all | solution.py:295
  23.0 0.8 %convert_add_fusion.packed_ref = f32[264,128]{1,0:T(8,128)S(1)} fusion(s32[1,64]{1,0:T(1,128)} %bitcast.10, bf16[128,128]{1,0:T(8,128)(2,1)} %bitcast.14, bf16[128,128]{1,0:T(8,128)(2,1)} %bitcast.15), kind=kLoop, calls=%fused_computation | loop fusion | flops 168960 | bytes 200960 | tf_op jit(solution)/shard_map/add | solution.py:307
  23.8 6.8 %grid_blocks.1.towers_ref = f32[4096,128]{1,0:T(8,128)S(1)} custom-call(s32[1]{0:T(128)} %bitcast.4.first_plane, f32[264,128]{1,0:T(8,128)S(1)} %convert_add_fusion.packed_ref), custom_call_target="tpu_custom_call" | custom-call | flops 300000000 | bytes 2200000 | tf_op jit(solution)/shard_map/grid_blocks/pallas_call | solution.py:315
  30.7 0.0 all-to-all-done
  30.7 0.0 copy-done
  30.7 0.0 copy-done.1
  30.7 0.0 copy-done.2
  30.7 1.9 %facet_sums.1 = bf16[32,32,128]{2,1,0:T(8,128)(2,1)S(1)} custom-call(s32[1]{0:T(128)} %bitcast.8.live, s32[1,64]{1,0:T(1,128)S(1)} %bitcast.12, s32[1,64]{1,0:T(1,128)S(1)} %bitcast.11, s32[128,12]{1,0:T(8,128)S(1)} %bitcast.9, bf16[4,128,128]{2,1,0:T(8,128)(2,1)S(1)} %copy-done, f32[4096,128]{1,0:T(8,128)S(1)} %grid_blocks.1.towers_ref), custom_call_target="tpu_custom_call" | custom-call | tf_op jit(solution)/shard_map/facet_sums/pallas_call | solution.py:338
  32.6 14.8 %all_to_all.15.in_ref = bf16[32,32,128]{2,1,0:T(8,128)(2,1)} all-to-all(bf16[32,32,128]{2,1,0:T(8,128)(2,1)S(1)} %facet_sums.1), channel_id=1, replica_groups={{0,1,2,3,4,5,6,7,8,9,10,11,12,13,14,15,16,17,18,19,20,21,22,23,24,25,26..., dimensions={0} | all-to-all | bytes 524288 | tf_op jit(solution)/shard_map/all_to_all | solution.py:357
  47.3 1.8 %plane_sums.1 = f32[32,128]{1,0:T(8,128)} custom-call(bf16[32,32,128]{2,1,0:T(8,128)(2,1)} %all_to_all.15.in_ref, bf16[4,128,256]{2,1,0:T(8,128)(2,1)} %constant.17.clone.shift_ref), custom_call_target="tpu_custom_call" | custom-call | tf_op jit(solution)/shard_map/plane_sums/pallas_call | solution.py:365
  49.2 13.6 %all_to_all.16 = f32[16,2,128]{2,1,0:T(2,128)S(1)} all-to-all(f32[16,2,128]{2,1,0:T(2,128)} %bitcast.13), channel_id=1, replica_groups={{256,288,320,352,384,416,448,480,0,32,64,96,128,160,192,224},{257,289,3..., dimensions={0} | all-to-all | bytes 32768 | tf_op jit(solution)/shard_map/all_to_all | solution.py:372
  62.7 0.6 reduce_sum.9
Async XLA Ops:
  0.0 30.7 %copy-start = (bf16[4,128,128]{2,1,0:T(8,128)(2,1)S(1)}, bf16[4,128,128]{2,1,0:T(8,128)(2,1)}, u32[]{:S(2)}) copy-start(bf16[4,128,128]{2,1,0:T(8,128)(2,1)} %constant.16.clone.shift_ref) | copy-start | bytes 393220
  0.0 30.7 %copy-start.1 = (s32[1,1,64]{2,1,0:T(1,128)S(1)}, s32[1,1,64]{2,1,0:T(1,128)}, u32[]{:S(2)}) copy-start(s32[1,1,64]{2,1,0:T(1,128)} %param.11) | copy-start | bytes 772
  0.0 30.7 %copy-start.2 = (s32[1,1,64,1]{2,3,1,0:T(1,128)S(1)}, s32[1,1,64,1]{2,3,1,0:T(1,128)}, u32[]{:S(2)}) copy-start(s32[1,1,64,1]{2,3,1,0:T(1,128)} %param.10) | copy-start | bytes 772
  1.4 29.3 %all-to-all-start = ((s32[64,2,12]{2,1,0:T(2,128)}), s32[64,2,12]{2,1,0:T(2,128)S(1)}, u32[]{:S(2)}, u32[]{:S(2)}) async-start(s32[64,2,12]{2,1,0:T(2,128)} %broadcast_in_dim.2), calls=%async_computation | async-start | bytes 131072 | tf_op jit(solution)/shard_map/all_to_all | solution.py:295

commit v3 on v2

--- a/solution.py
+++ b/solution.py
@@ -25,10 +25,11 @@
 CELL_STEP = 0.37
 WTERM_LIMIT = 4000.0
 SCALE = 1.0 / math.sqrt(BLOCK_VISIBILITY * N_COL * N_WA * DEVICE_SLOTS)
-UNROLL = 4
+CELLS = DEVICE_COLUMNS * COLUMN_SUBGRIDS * RANGE_PLANES
+UNROLL = 8
 GROUP = 32
 TOUCH_Z, TOUCH_X = 10, 2
-PLANE_X, PLANE_WA = 0, 0
+PLANE_X, PLANE_WA = 2, 4
 LINE_Z = 8
 
 f32 = jnp.float32
@@ -63,10 +64,51 @@
     return 1.0 - 2.0 * (sine * sine), 2.0 * (sine * cosine)
 
 
+def plane_place(k):
+    return ((k // N_WA + PLANE_X) % 4) * N_WA + (k + PLANE_WA) % N_WA
+
+
+def plane_group():
+    return [plane_place(k) for k in range(GROUP)]
+
+
+def line_group():
+    return [(z + LINE_Z) % FACETS for z in range(FACETS)]
+
+
+def shift_parts(difference, d):
+    h = (difference.astype(f32) - d) * (1.0 / S)
+    h = h - jnp.floor(h + 0.5)
+    z = h * h
+    cotangent = horner(COSINE_FIT, z) / (h * horner(SINE_FIT, z))
+    scale = jnp.where(difference & 1 == 0, -math.sin(math.pi * d) / S, math.sin(math.pi * d) / S)
+    return scale * cotangent, -scale
+
+
+def make_shifts(left_ref, right_ref):
+    r = lax.broadcasted_iota(jnp.int32, (S, 2 * S), 0)
+    lane = lax.broadcasted_iota(jnp.int32, (S, 2 * S), 1)
+    x = 2 * plane_place(r & (GROUP - 1)) + r // GROUP
+    for fx in range(4):
+        real, imag = shift_parts(x - (lane & (S - 1)), (fx + 0.5) / 4)
+        high, low = split_bf16(jnp.where(lane < S, real, imag) * SCALE)
+        left_ref[fx] = jnp.concatenate([high, low], axis=0)
+    m = lax.broadcasted_iota(jnp.int32, (2 * S, 2 * S), 0)
+    lane = lax.broadcasted_iota(jnp.int32, (2 * S, 2 * S), 1)
+    for fy in range(4):
+        real, imag = shift_parts((lane & (S - 1)) - (m & (S - 1)), (fy + 0.5) / 4)
+        imag = jnp.where(m < S, imag, -imag)
+        high, low = split_bf16(jnp.where((m < S) == (lane < S), real, imag))
+        right_ref[fy] = jnp.concatenate([high, low], axis=1)
+
+
 def grid_kernel(
-    first_plane,
     packed_ref,
     out_ref,
+    phase_ref,
+    chosen_ref,
+    left_ref,
+    right_ref,
     cell_row,
     cells,
     vis_rows,
@@ -75,9 +117,35 @@
     screen_b,
     arrival,
 ):
-    cell_row[...] = packed_ref[4 * DEVICE_SLOTS : 4 * DEVICE_SLOTS + 8, :].astype(jnp.int32)
+    labels = packed_ref[4 * DEVICE_SLOTS : 4 * DEVICE_SLOTS + 8, :].astype(jnp.int32)
+    cell_row[...] = labels
     copy = pltpu.make_async_copy(cell_row, cells, arrival)
     copy.start()
+    label = labels[0:1, :DEVICE_SLOTS]
+    owner = labels[1:2, :DEVICE_SLOTS]
+    column_half = (label // (COLUMN_SUBGRIDS * RANGE_PLANES)) % DEVICE_COLUMNS
+    row = (label // RANGE_PLANES) % COLUMN_SUBGRIDS
+    column = owner * DEVICE_COLUMNS + column_half
+    columns = DEVICE_COLUMNS * N_COL
+
+    facet = lax.broadcasted_iota(jnp.int32, (FACETS, 1), 0)
+    fx = (facet % 4).astype(f32)
+    fy = (facet // 4).astype(f32)
+    turns = CELL_STEP * (
+        (column.astype(f32) - columns / 2 + 0.5) * ((fx - 1.5) / 4)
+        + (row.astype(f32) - COLUMN_SUBGRIDS / 2 + 0.5) * ((fy - 1.5) / 4)
+    )
+    cosine, sine = cos_sin_turns(turns)
+    phase_ref[:FACETS] = cosine
+    phase_ref[FACETS:] = sine
+
+    place = ((owner // 4 + 16 - TOUCH_Z) % 16) * 4 + (owner + 4 - TOUCH_X) % 4
+    place = place * DEVICE_COLUMNS + column_half
+    chosen = lax.broadcasted_iota(jnp.int32, (columns, DEVICE_SLOTS), 0) == place
+    alive = lax.broadcasted_iota(jnp.int32, (1, DEVICE_SLOTS), 1) < labels[2:3, :DEVICE_SLOTS]
+    chosen_ref[...] = jnp.where(chosen & alive, 1.0, 0.0).astype(bf16)
+
+    make_shifts(left_ref, right_ref)
     vis_rows[...] = packed_ref[: 2 * DEVICE_SLOTS, :]
     uv_rows[...] = packed_ref[2 * DEVICE_SLOTS : 4 * DEVICE_SLOTS, :]
 
@@ -88,9 +156,10 @@
     lag = -radius / (1.0 + jnp.sqrt(1.0 - radius))
     sign = jnp.where(lane < S, -1.0, 1.0).astype(f32)
     plane_step = 2.0 * WTERM_LIMIT / (RANGE_PLANES * N_WA)
+    first_plane = labels[0:1, :] // CELLS * RANGE_PLANES
 
     def make_screen(p, carry):
-        depth = -WTERM_LIMIT + ((first_plane[0] + p).astype(f32) + 0.5) * plane_step
+        depth = -WTERM_LIMIT + ((first_plane + p).astype(f32) + 0.5) * plane_step
         cosine, sine = cos_sin_turns(depth * lag)
         screen_a[p] = cosine
         screen_b[p] = sine * sign
@@ -147,33 +216,20 @@
     return high, (x - high.astype(f32)).astype(bf16)
 
 
-def facet_kernel(live, owner_ref, cell_ref, touch_ref, shift_ref, towers_ref, out_ref, facet_ref, rows_ref):
-    cell = cell_ref[...]
-    column = owner_ref[...] * DEVICE_COLUMNS + cell // (COLUMN_SUBGRIDS * RANGE_PLANES)
-    row = (cell // RANGE_PLANES) % COLUMN_SUBGRIDS
-    facet = lax.broadcasted_iota(jnp.int32, (FACETS, 1), 0)
-    fx = (facet % 4).astype(f32)
-    fy = (facet // 4).astype(f32)
+def facet_kernel(
+    phase_ref, chosen_ref, touch_ref, left_ref, right_ref, towers_ref, out_ref, facet_ref, rows_ref
+):
     columns = DEVICE_COLUMNS * N_COL
-    turns = CELL_STEP * (
-        (column.astype(f32) - columns / 2 + 0.5) * ((fx - 1.5) / 4)
-        + (row.astype(f32) - COLUMN_SUBGRIDS / 2 + 0.5) * ((fy - 1.5) / 4)
-    )
-    cosine, sine = cos_sin_turns(turns)
-    named = touch_ref[...]
-    facet_lane = lax.broadcasted_iota(jnp.int32, (columns, FACETS), 1)
+    named = touch_ref[...].astype(f32)
+    facet_lane = lax.broadcasted_iota(jnp.int32, (columns, FACETS), 1).astype(f32)
     touched = named[:, 0:1] == facet_lane
     for t in range(1, TOUCH):
         touched = touched | (named[:, t : t + 1] == facet_lane)
     touched = jnp.where(touched, 1.0, 0.0).astype(bf16)
-    owner = owner_ref[...]
-    place = ((owner // 4 + 16 - TOUCH_Z) % 16) * 4 + (owner + 4 - TOUCH_X) % 4
-    place = place * DEVICE_COLUMNS + cell // (COLUMN_SUBGRIDS * RANGE_PLANES)
-    chosen = lax.broadcasted_iota(jnp.int32, (columns, DEVICE_SLOTS), 0) == place
-    alive = lax.broadcasted_iota(jnp.int32, (columns, DEVICE_SLOTS), 1) < live[0]
-    chosen = jnp.where(chosen & alive, 1.0, 0.0).astype(bf16)
-    mask = lax.dot_general(touched, chosen, (((0,), (0,)), ((), ())), preferred_element_type=f32)
-    weights = jnp.concatenate([cosine * mask, sine * mask], axis=0)
+    mask = lax.dot_general(
+        touched, chosen_ref[...], (((0,), (0,)), ((), ())), preferred_element_type=f32
+    )
+    weights = phase_ref[...] * jnp.concatenate([mask, mask], axis=0)
     high, low = split_bf16(weights)
     left = jnp.concatenate(
         [jnp.concatenate([high, high], axis=1), jnp.concatenate([low, jnp.zeros_like(low)], axis=1)],
@@ -206,80 +262,25 @@
             [jnp.concatenate(plain, axis=1), jnp.concatenate(turned, axis=1)], axis=0
         )
         high, low = split_bf16(stack)
-        shift = shift_ref[fx]
+        shift = left_ref[fx]
         first = jnp.dot(shift, high, preferred_element_type=f32)
         second = jnp.dot(shift[:S], low, preferred_element_type=f32)
-        image = first[:S] + first[S:] + second
+        half = first[:S] + first[S:] + second
         for fy in range(4):
+            high, low = split_bf16(half[:, 2 * S * fy : 2 * S * (fy + 1)])
+            products = jnp.dot(
+                jnp.concatenate([high, low], axis=0), right_ref[fy], preferred_element_type=f32
+            )
+            image = products[:S, : 2 * S] + products[:S, 2 * S :] + products[S:, : 2 * S]
             place = (fx + 4 * fy - LINE_Z) % FACETS
             for i in range(2):
                 rows_ref[pl.ds(2 * place + i, GROUP, stride=GROUP), :] = image[
-                    GROUP * i : GROUP * (i + 1), 2 * S * fy : 2 * S * (fy + 1)
+                    GROUP * i : GROUP * (i + 1)
                 ]
     out_ref[...] = rows_ref[...].astype(bf16).reshape(GROUP, GROUP, 2 * S)
 
 
-def shift_matrix(d):
-    k = np.arange(S) - S // 2
-    x = np.arange(S)
-    return np.exp(2j * np.pi * k * x[:, None] / S) @ np.exp(-2j * np.pi * k[:, None] * (x + d) / S) / S
-
-
-def plane_group():
-    return [
-        ((x + PLANE_X) % 4) * N_WA + (wa + PLANE_WA) % N_WA for x in range(4) for wa in range(N_WA)
-    ]
-
-
-def line_group():
-    return [(z + LINE_Z) % FACETS for z in range(FACETS)]
-
-
-def left_shifts():
-    order = np.array([2 * dest + i for i in range(2) for dest in plane_group()])
-    tables = []
-    for fx in range(4):
-        shift = shift_matrix((fx + 0.5) / 4)[order] * SCALE
-        table = np.concatenate([shift.real, shift.imag], axis=1).astype(np.float32)
-        high = table.astype(jnp.bfloat16)
-        low = (table - high.astype(np.float32)).astype(jnp.bfloat16)
-        tables.append(np.concatenate([high, low], axis=0))
-    return np.stack(tables)
-
-
-def right_shifts():
-    tables = []
-    for fy in range(4):
-        shift = shift_matrix((fy + 0.5) / 4).T
-        tables.append(
-            np.concatenate(
-                [
-                    np.concatenate([shift.real, shift.imag], axis=1),
-                    np.concatenate([-shift.imag, shift.real], axis=1),
-                ],
-                axis=0,
-            )
-        )
-    table = np.stack(tables).astype(np.float32)
-    high = table.astype(jnp.bfloat16)
-    return np.concatenate([high, (table - high.astype(np.float32)).astype(jnp.bfloat16)], axis=2)
-
-
-def middle_kernel(in_ref, shift_ref, out_ref):
-    total = in_ref[0].astype(f32)
-    for k in range(1, GROUP):
-        total = total + in_ref[k].astype(f32)
-    for fy in range(4):
-        high, low = split_bf16(total[8 * fy : 8 * (fy + 1)])
-        both = jnp.concatenate([high, low], axis=0)
-        products = jnp.dot(both, shift_ref[(fy + LINE_Z // 4) % 4], preferred_element_type=f32)
-        out_ref[8 * fy : 8 * (fy + 1), :] = (
-            products[:8, : 2 * S] + products[:8, 2 * S :] + products[8:, : 2 * S]
-        )
-
-
 VMEM = pl.BlockSpec(memory_space=pltpu.VMEM)
-SMEM = pl.BlockSpec(memory_space=pltpu.SMEM)
 
 
 def shards(
@@ -293,7 +294,7 @@
     range_index = lax.axis_index("wa")
     touch_group = [((z + TOUCH_Z) % 16) * 4 + (x + TOUCH_X) % 4 for z in range(16) for x in range(4)]
     named = lax.all_to_all(
-        jnp.broadcast_to(touch_lists[None], (N_COL, DEVICE_COLUMNS, TOUCH)),
+        jnp.broadcast_to(touch_lists[None].astype(bf16), (N_COL, DEVICE_COLUMNS, TOUCH)),
         ("z", "x"),
         split_axis=0,
         concat_axis=0,
@@ -303,20 +304,29 @@
     cells = block_cell_number.reshape(1, DEVICE_SLOTS)
     shape = 4 * DEVICE_SLOTS + 8
     half = 2 * DEVICE_SLOTS
+    lanes = (0, BLOCK_VISIBILITY - DEVICE_SLOTS)
+    row = lax.broadcasted_iota(jnp.int32, (shape, BLOCK_VISIBILITY), 0)
     packed = (
         jnp.pad(visibilities.reshape(half, BLOCK_VISIBILITY), ((0, shape - half), (0, 0))).astype(f32)
         + jnp.pad(
             visibility_uv_offsets.reshape(half, BLOCK_VISIBILITY), ((half, 8), (0, 0))
         ).astype(f32)
-        + jnp.pad(
-            cells, ((2 * half, 7), (0, BLOCK_VISIBILITY - DEVICE_SLOTS))
-        ).astype(f32)
-    )
-    towers = pl.pallas_call(
+        + jnp.pad(cells, ((2 * half, 7), lanes)).astype(f32)
+        + jnp.pad(block_owner_index.reshape(1, DEVICE_SLOTS), ((2 * half + 1, 6), lanes)).astype(f32)
+        + jnp.where(row == 2 * half, (CELLS * range_index).astype(f32), 0.0)
+        + jnp.where(row == 2 * half + 2, live_counts[0, 0].astype(f32), 0.0)
+    )
+    towers, phases, chosen, left, right = pl.pallas_call(
         grid_kernel,
-        out_shape=jax.ShapeDtypeStruct((S * DEVICE_SLOTS, 2 * S), f32),
-        in_specs=[SMEM, VMEM],
-        out_specs=VMEM,
+        out_shape=(
+            jax.ShapeDtypeStruct((S * DEVICE_SLOTS, 2 * S), f32),
+            jax.ShapeDtypeStruct((2 * FACETS, DEVICE_SLOTS), f32),
+            jax.ShapeDtypeStruct((DEVICE_COLUMNS * N_COL, DEVICE_SLOTS), bf16),
+            jax.ShapeDtypeStruct((4, 2 * S, 2 * S), bf16),
+            jax.ShapeDtypeStruct((4, 2 * S, 4 * S), bf16),
+        ),
+        in_specs=[VMEM],
+        out_specs=(VMEM,) * 5,
         scratch_shapes=[
             pltpu.VMEM((8, BLOCK_VISIBILITY), jnp.int32),
             pltpu.SMEM((8, BLOCK_VISIBILITY), jnp.int32),
@@ -332,13 +342,12 @@
         ),
         name="grid_blocks",
     )(
-        (range_index * RANGE_PLANES).reshape(1).astype(jnp.int32),
         packed,
     )
     partial_rows = pl.pallas_call(
         facet_kernel,
         out_shape=jax.ShapeDtypeStruct((GROUP, GROUP, 2 * S), bf16),
-        in_specs=[SMEM, VMEM, VMEM, VMEM, VMEM, VMEM],
+        in_specs=[VMEM] * 6,
         out_specs=VMEM,
         scratch_shapes=[
             pltpu.VMEM((FACETS * S, 2 * S), f32),
@@ -347,11 +356,11 @@
         compiler_params=pltpu.CompilerParams(vmem_limit_bytes=24 * 1024 * 1024),
         name="facet_sums",
     )(
-        live_counts.reshape(1),
-        block_owner_index.reshape(1, DEVICE_SLOTS),
-        cells,
+        phases,
+        chosen,
         named,
-        jnp.asarray(left_shifts()),
+        left,
+        right,
         towers,
     )
     arrived = lax.all_to_all(
@@ -362,13 +371,7 @@
         axis_index_groups=[plane_group()],
         tiled=True,
     )
-    plane_rows = pl.pallas_call(
-        middle_kernel,
-        out_shape=jax.ShapeDtypeStruct((GROUP, 2 * S), f32),
-        in_specs=[VMEM, VMEM],
-        out_specs=VMEM,
-        name="plane_sums",
-    )(arrived, jnp.asarray(right_shifts()))
+    plane_rows = jnp.sum(arrived.astype(f32), axis=0)
     arrived = lax.all_to_all(
         plane_rows.reshape(FACETS, 2, 2 * S),
         "z",

time: 63.6 us -> 59.7 us (0.939)
  Pallas kernels: 10.5 us -> 8.06 us
  blocking collectives: 28.3 us -> 26.4 us
  other arithmetic: 1.39 us -> 2.26 us
  local copies, waits for them, and re-layouts: 1.36 us -> 0.62 us
    pallas_call x2 -> x1, Pallas kernels: 8.63 us -> 5.69 us  [shards(): pl.pallas_call(grid_kernel, out_shape=(jax.ShapeDtypeStruct((S * DEVICE_S...]
    all_to_all x1, blocking collectives: 14.8 us -> 13.1 us  [shards(): lax.all_to_all(partial_rows, ('x', 'wa'), split_axis=0, concat_axis=0, ax...]
    broadcast_in_dim x1, local copies, waits for them, and re-layouts: 1.34 us -> 0.62 us  [shards(): jnp.broadcast_to(touch_lists[None].astype(bf16), (N_COL, DEVICE_COLUMNS,...]
    convert_element_type x0 -> x1, other arithmetic: none -> 0.68 us  [shards(): touch_lists[None].astype(bf16)]
  transfers between devices with their start and end apart: 1 -> 1, of which waited for: 0 -> 0; matrix products, arithmetic and copies ran while one was open for 1% -> 2% of each run, Pallas kernels for 11% -> 10%
where the time goes in v3:
time: 59.7 us; the launch traced here: 59.1 us
  blocking collectives  26.4 us (44%)
  starting transfers between devices  21 us (35%)
  Pallas kernels  8.06 us (14%)
  other arithmetic  2.26 us (4%)
  between operations  0.7 us (1%)
  local copies, waits for them, and re-layouts  0.62 us (1%)
    all_to_all x1, starting transfers between devices, shards(): lax.all_to_all(jnp.broadcast_to(touch_lists[None].astype(bf16), (N_COL, D...  21 us
    all_to_all x1, blocking collectives, shards(): lax.all_to_all(plane_rows.reshape(FACETS, 2, 2 * S), 'z', split_axis=0, c...  13.4 us
    all_to_all x1, blocking collectives, shards(): lax.all_to_all(partial_rows, ('x', 'wa'), split_axis=0, concat_axis=0, ax...  13.1 us
    pallas_call x1, Pallas kernels, shards(): pl.pallas_call(grid_kernel, out_shape=(jax.ShapeDtypeStruct((S * DEVICE_S...  5.69 us
    pallas_call x1, Pallas kernels, shards(): pl.pallas_call(facet_kernel, out_shape=jax.ShapeDtypeStruct((GROUP, GROUP...  2.37 us
  transfers between devices with their start and end apart: 1, of which 0 were waited for; matrix products, arithmetic and copies ran while one was open for 2% of the time, Pallas kernels for 10%

profile of v3, /device:TPU:1, one launch (start us, length us, event | category | flops | bytes accessed | tf_op | source)
XLA Modules:
  0.0 59.1 jit_solution(6016456936529125827)
XLA Ops:
  0.0 0.7 %convert_element_type.39 = bf16[2,12]{1,0:T(2,128)(2,1)S(1)} convert(s32[2,12]{1,0:T(2,128)} %param.11) | non-fusion elementwise | flops 24 | bytes 144 | tf_op jit(solution)/shard_map/convert_element_type | solution.py:297
  0.7 0.6 %broadcast_in_dim.21 = bf16[64,2,12]{2,1,0:T(2,128)(2,1)} broadcast(bf16[2,12]{1,0:T(2,128)(2,1)S(1)} %convert_element_type.39), dimensions={1,2} | broadcast | bytes 3120 | tf_op jit(solution)/shard_map/broadcast_in_dim | solution.py:297
  1.3 21.0 %all-to-all-start = ((bf16[64,2,12]{2,1,0:T(2,128)(2,1)}), bf16[64,2,12]{2,1,0:T(2,128)(2,1)S(1)}, u32[]{:S(2)}, u32[]{:S(2)}) async-start(bf16[64,2,12]{2,1,0:T(2,128)(2,1)} %broadcast_in_dim.21), calls=%async_computation | async-start | bytes 65536 | tf_op jit(solution)/shard_map/all_to_all | solution.py:296
  23.0 0.9 %add_add_fusion.packed_ref = f32[264,128]{1,0:T(8,128)S(1)} fusion(s32[1,64]{1,0:T(1,128)} %bitcast.11, s32[1,64]{1,0:T(1,128)} %bitcast.12, f32[264]{0:T(512)S(1)} %get-tuple-element.16, f32[264]{0:T(512)S(1)} %get-tuple-element.15, bf16[128,128]{1,0:T(8,128)(2,1)} %bitcast.9, bf16[128,128]{1,0:T(8,128)(2,1)} %bitcast.10), kind=kLoop, calls=%fused_computation.1 | loop fusion | flops 304128 | bytes 203328 | tf_op jit(solution)/shard_map/add | solution.py:310
  23.9 5.7 %grid_blocks.1 = (f32[4096,128]{1,0:T(8,128)S(1)}, f32[32,64]{1,0:T(8,128)S(1)}, bf16[128,64]{1,0:T(8,128)(2,1)S(1)}, bf16[4,128,128]{2,1,0:T(8,128)(2,1)S(1)}, bf16[4,128,256]{2,1,0:T(8,128)(2,1)S(1)}) custom-call(f32[264,128]{1,0:T(8,128)S(1)} %add_add_fusion.packed_ref), custom_call_target="tpu_custom_call" | custom-call | flops 300000000 | bytes 2200000 | tf_op jit(solution)/shard_map/grid_blocks/pallas_call | solution.py:319
  29.6 0.0 all-to-all-done
  29.7 2.4 %facet_sums.1 = bf16[32,32,128]{2,1,0:T(8,128)(2,1)S(1)} custom-call(f32[32,64]{1,0:T(8,128)S(1)} %get-tuple-element.10.phase_ref, bf16[128,64]{1,0:T(8,128)(2,1)S(1)} %get-tuple-element.11.chosen_ref, bf16[128,12]{1,0:T(8,128)(2,1)S(1)} %bitcast.7, bf16[4,128,128]{2,1,0:T(8,128)(2,1)S(1)} %get-tuple-element.12.left_ref, ...), custom_call_target="tpu_custom_call" | custom-call | tf_op jit(solution)/shard_map/facet_sums/pallas_call | solution.py:347
  32.0 13.1 %all_to_all.15 = bf16[32,32,128]{2,1,0:T(8,128)(2,1)S(1)} all-to-all(bf16[32,32,128]{2,1,0:T(8,128)(2,1)S(1)} %facet_sums.1), channel_id=1, replica_groups={{20,21,22,23,16,17,18,19,28,29,30,31,24,25,26,27,4,5,6,7,0,1,2,3,12,13,..., dimensions={0} | all-to-all | bytes 524288 | tf_op jit(solution)/shard_map/all_to_all | solution.py:366
  45.1 13.4 %all_to_all.16 = f32[16,2,128]{2,1,0:T(2,128)S(1)} all-to-all(f32[16,2,128]{2,1,0:T(2,128)S(1)} %bitcast.8), channel_id=1, replica_groups={{256,288,320,352,384,416,448,480,0,32,64,96,128,160,192,224},{257,289,3..., dimensions={0} | all-to-all | bytes 32768 | tf_op jit(solution)/shard_map/all_to_all | solution.py:375
  58.5 0.6 reduce_sum.19
  (2 shorter events, 0.1 us)
Async XLA Ops:
  1.3 28.3 %all-to-all-start = ((bf16[64,2,12]{2,1,0:T(2,128)(2,1)}), bf16[64,2,12]{2,1,0:T(2,128)(2,1)S(1)}, u32[]{:S(2)}, u32[]{:S(2)}) async-start(bf16[64,2,12]{2,1,0:T(2,128)(2,1)} %broadcast_in_dim.21), calls=%async_computation | async-start | bytes 65536 | tf_op jit(solution)/shard_map/all_to_all | solution.py:296

commit v4 on v3

--- a/solution.py
+++ b/solution.py
@@ -25,10 +25,9 @@
 CELL_STEP = 0.37
 WTERM_LIMIT = 4000.0
 SCALE = 1.0 / math.sqrt(BLOCK_VISIBILITY * N_COL * N_WA * DEVICE_SLOTS)
-CELLS = DEVICE_COLUMNS * COLUMN_SUBGRIDS * RANGE_PLANES
 UNROLL = 8
 GROUP = 32
-TOUCH_Z, TOUCH_X = 10, 2
+TOUCH_Z, TOUCH_X = 11, 2
 PLANE_X, PLANE_WA = 2, 4
 LINE_Z = 8
 
@@ -40,7 +39,7 @@
     nodes = np.cos(np.pi * (np.arange(400) + 0.5) / 400) * 0.125 + 0.125
     root = np.sqrt(nodes)
     sine = np.polynomial.chebyshev.Chebyshev.fit(nodes, np.sin(np.pi * root) / root, 4, domain=[0, 0.25])
-    cosine = np.polynomial.chebyshev.Chebyshev.fit(nodes, np.cos(np.pi * root), 5, domain=[0, 0.25])
+    cosine = np.polynomial.chebyshev.Chebyshev.fit(nodes, np.cos(np.pi * root), 4, domain=[0, 0.25])
     return tuple(
         [float(c) for c in fit.convert(kind=np.polynomial.Polynomial).coef] for fit in (sine, cosine)
     )
@@ -142,7 +141,7 @@
     place = ((owner // 4 + 16 - TOUCH_Z) % 16) * 4 + (owner + 4 - TOUCH_X) % 4
     place = place * DEVICE_COLUMNS + column_half
     chosen = lax.broadcasted_iota(jnp.int32, (columns, DEVICE_SLOTS), 0) == place
-    alive = lax.broadcasted_iota(jnp.int32, (1, DEVICE_SLOTS), 1) < labels[2:3, :DEVICE_SLOTS]
+    alive = lax.broadcasted_iota(jnp.int32, (1, DEVICE_SLOTS), 1) < labels[2:3, 0:1]
     chosen_ref[...] = jnp.where(chosen & alive, 1.0, 0.0).astype(bf16)
 
     make_shifts(left_ref, right_ref)
@@ -156,11 +155,12 @@
     lag = -radius / (1.0 + jnp.sqrt(1.0 - radius))
     sign = jnp.where(lane < S, -1.0, 1.0).astype(f32)
     plane_step = 2.0 * WTERM_LIMIT / (RANGE_PLANES * N_WA)
-    first_plane = labels[0:1, :] // CELLS * RANGE_PLANES
+    first_plane = (labels[3:4, 0:1] * RANGE_PLANES).astype(f32)
+    first_turns = (-WTERM_LIMIT + (first_plane + 0.5) * plane_step) * lag
+    step_turns = plane_step * lag
 
     def make_screen(p, carry):
-        depth = -WTERM_LIMIT + ((first_plane + p).astype(f32) + 0.5) * plane_step
-        cosine, sine = cos_sin_turns(depth * lag)
+        cosine, sine = cos_sin_turns(first_turns + p.astype(f32) * step_turns)
         screen_a[p] = cosine
         screen_b[p] = sine * sign
         return carry
@@ -254,9 +254,16 @@
                 part[:FACETS] + sign * pltpu.roll(part[FACETS:], S, 1)
             )
 
+    shifted = []
+    for fy in range(4):
+        high, low = split_bf16(facet_ref[4 * S * fy : 4 * S * (fy + 1), :])
+        first = jnp.dot(high, right_ref[fy], preferred_element_type=f32)
+        second = jnp.dot(low, right_ref[fy, :, : 2 * S], preferred_element_type=f32)
+        shifted.append(first[:, : 2 * S] + first[:, 2 * S :] + second)
+
     wide = jnp.where(lax.broadcasted_iota(jnp.int32, (S, 2 * S), 1) < S, -1.0, 1.0).astype(f32)
     for fx in range(4):
-        plain = [facet_ref[(fx + 4 * fy) * S : (fx + 4 * fy + 1) * S, :] for fy in range(4)]
+        plain = [rows[S * fx : S * (fx + 1)] for rows in shifted]
         turned = [wide * pltpu.roll(g, S, 1) for g in plain]
         stack = jnp.concatenate(
             [jnp.concatenate(plain, axis=1), jnp.concatenate(turned, axis=1)], axis=0
@@ -265,17 +272,12 @@
         shift = left_ref[fx]
         first = jnp.dot(shift, high, preferred_element_type=f32)
         second = jnp.dot(shift[:S], low, preferred_element_type=f32)
-        half = first[:S] + first[S:] + second
+        image = first[:S] + first[S:] + second
         for fy in range(4):
-            high, low = split_bf16(half[:, 2 * S * fy : 2 * S * (fy + 1)])
-            products = jnp.dot(
-                jnp.concatenate([high, low], axis=0), right_ref[fy], preferred_element_type=f32
-            )
-            image = products[:S, : 2 * S] + products[:S, 2 * S :] + products[S:, : 2 * S]
             place = (fx + 4 * fy - LINE_Z) % FACETS
             for i in range(2):
                 rows_ref[pl.ds(2 * place + i, GROUP, stride=GROUP), :] = image[
-                    GROUP * i : GROUP * (i + 1)
+                    GROUP * i : GROUP * (i + 1), 2 * S * fy : 2 * S * (fy + 1)
                 ]
     out_ref[...] = rows_ref[...].astype(bf16).reshape(GROUP, GROUP, 2 * S)
 
@@ -305,7 +307,6 @@
     shape = 4 * DEVICE_SLOTS + 8
     half = 2 * DEVICE_SLOTS
     lanes = (0, BLOCK_VISIBILITY - DEVICE_SLOTS)
-    row = lax.broadcasted_iota(jnp.int32, (shape, BLOCK_VISIBILITY), 0)
     packed = (
         jnp.pad(visibilities.reshape(half, BLOCK_VISIBILITY), ((0, shape - half), (0, 0))).astype(f32)
         + jnp.pad(
@@ -313,8 +314,11 @@
         ).astype(f32)
         + jnp.pad(cells, ((2 * half, 7), lanes)).astype(f32)
         + jnp.pad(block_owner_index.reshape(1, DEVICE_SLOTS), ((2 * half + 1, 6), lanes)).astype(f32)
-        + jnp.where(row == 2 * half, (CELLS * range_index).astype(f32), 0.0)
-        + jnp.where(row == 2 * half + 2, live_counts[0, 0].astype(f32), 0.0)
+        + jnp.pad(live_counts, ((2 * half + 2, 5), (0, BLOCK_VISIBILITY - 1))).astype(f32)
+        + jnp.pad(
+            range_index.reshape(1, 1).astype(jnp.int32),
+            ((2 * half + 3, 4), (0, BLOCK_VISIBILITY - 1)),
+        ).astype(f32)
     )
     towers, phases, chosen, left, right = pl.pallas_call(
         grid_kernel,

time: 59.7 us -> 58.2 us (0.975)
  starting transfers between devices: 21 us -> 20.1 us
    all_to_all x1, starting transfers between devices: 21 us -> 20.1 us  [shards(): lax.all_to_all(jnp.broadcast_to(touch_lists[None].astype(bf16), (N_COL, D...]
  transfers between devices with their start and end apart: 1 -> 1, of which waited for: 0 -> 0; matrix products, arithmetic and copies ran while one was open for 2% -> 1% of each run, Pallas kernels for 10% -> 10%
where the time goes in v4:
time: 58.2 us; the launch traced here: 57.5 us
  blocking collectives  26.5 us (46%)
  starting transfers between devices  20.1 us (35%)
  Pallas kernels  7.51 us (13%)
  other arithmetic  2.14 us (4%)
  between operations  0.69 us (1%)
  local copies, waits for them, and re-layouts  0.62 us (1%)
    all_to_all x1, starting transfers between devices, shards(): lax.all_to_all(jnp.broadcast_to(touch_lists[None].astype(bf16), (N_COL, D...  20.1 us
    all_to_all x1, blocking collectives, shards(): lax.all_to_all(plane_rows.reshape(FACETS, 2, 2 * S), 'z', split_axis=0, c...  13.4 us
    all_to_all x1, blocking collectives, shards(): lax.all_to_all(partial_rows, ('x', 'wa'), split_axis=0, concat_axis=0, ax...  13.1 us
    pallas_call x1, Pallas kernels, shards(): pl.pallas_call(grid_kernel, out_shape=(jax.ShapeDtypeStruct((S * DEVICE_S...  5.52 us
    pallas_call x1, Pallas kernels, shards(): pl.pallas_call(facet_kernel, out_shape=jax.ShapeDtypeStruct((GROUP, GROUP...  1.99 us
  transfers between devices with their start and end apart: 1, of which 0 were waited for; matrix products, arithmetic and copies ran while one was open for 1% of the time, Pallas kernels for 10%

profile of v4, /device:TPU:1, one launch (start us, length us, event | category | flops | bytes accessed | tf_op | source)
XLA Modules:
  0.0 57.5 jit_solution(15432724546718452371)
XLA Ops:
  0.0 0.7 %convert_element_type.35 = bf16[2,12]{1,0:T(2,128)(2,1)S(1)} convert(s32[2,12]{1,0:T(2,128)} %param.11) | non-fusion elementwise | flops 24 | bytes 144 | tf_op jit(solution)/shard_map/convert_element_type | solution.py:299
  0.7 0.6 %broadcast_in_dim.2 = bf16[64,2,12]{2,1,0:T(2,128)(2,1)} broadcast(bf16[2,12]{1,0:T(2,128)(2,1)S(1)} %convert_element_type.35), dimensions={1,2} | broadcast | bytes 3120 | tf_op jit(solution)/shard_map/broadcast_in_dim | solution.py:299
  1.3 20.1 %all-to-all-start = ((bf16[64,2,12]{2,1,0:T(2,128)(2,1)}), bf16[64,2,12]{2,1,0:T(2,128)(2,1)S(1)}, u32[]{:S(2)}, u32[]{:S(2)}) async-start(bf16[64,2,12]{2,1,0:T(2,128)(2,1)} %broadcast_in_dim.2), calls=%async_computation | async-start | bytes 65536 | tf_op jit(solution)/shard_map/all_to_all | solution.py:298
  22.1 0.8 %convert_add_fusion.packed_ref = f32[264,128]{1,0:T(8,128)S(1)} fusion(s32[1,1]{1,0:T(1,128)} %bitcast.4, s32[1,1]{1,0:T(1,128)S(6)} %copy.9, s32[1,64]{1,0:T(1,128)} %bitcast.11, s32[1,64]{1,0:T(1,128)} %bitcast.12, bf16[128,128]{1,0:T(8,128)(2,1)} %bitcast.9, bf16[128,128]{1,0:T(8,128)(2,1)} %bitcast.10), kind=kLoop, calls=%fused_computation.1 | loop fusion | flops 371712 | bytes 201224 | tf_op jit(solution)/shard_map/add | solution.py:311
  22.9 5.5 %grid_blocks.1 = (f32[4096,128]{1,0:T(8,128)S(1)}, f32[32,64]{1,0:T(8,128)S(1)}, bf16[128,64]{1,0:T(8,128)(2,1)S(1)}, bf16[4,128,128]{2,1,0:T(8,128)(2,1)S(1)}, bf16[4,128,256]{2,1,0:T(8,128)(2,1)S(1)}) custom-call(f32[264,128]{1,0:T(8,128)S(1)} %convert_add_fusion.packed_ref), custom_call_target="tpu_custom_call" | custom-call | flops 300000000 | bytes 2200000 | tf_op jit(solution)/shard_map/grid_blocks/pallas_call | solution.py:323
  28.4 0.0 all-to-all-done
  28.4 2.0 %facet_sums.1 = bf16[32,32,128]{2,1,0:T(8,128)(2,1)S(1)} custom-call(f32[32,64]{1,0:T(8,128)S(1)} %get-tuple-element.10.phase_ref, bf16[128,64]{1,0:T(8,128)(2,1)S(1)} %get-tuple-element.11.chosen_ref, bf16[128,12]{1,0:T(8,128)(2,1)S(1)} %bitcast.7, bf16[4,128,128]{2,1,0:T(8,128)(2,1)S(1)} %get-tuple-element.12.left_ref, ...), custom_call_target="tpu_custom_call" | custom-call | tf_op jit(solution)/shard_map/facet_sums/pallas_call | solution.py:351
  30.4 13.1 %all_to_all.15 = bf16[32,32,128]{2,1,0:T(8,128)(2,1)S(1)} all-to-all(bf16[32,32,128]{2,1,0:T(8,128)(2,1)S(1)} %facet_sums.1), channel_id=1, replica_groups={{20,21,22,23,16,17,18,19,28,29,30,31,24,25,26,27,4,5,6,7,0,1,2,3,12,13,..., dimensions={0} | all-to-all | bytes 524288 | tf_op jit(solution)/shard_map/all_to_all | solution.py:370
  43.5 13.4 %all_to_all.16 = f32[16,2,128]{2,1,0:T(2,128)S(1)} all-to-all(f32[16,2,128]{2,1,0:T(2,128)S(1)} %bitcast.8), channel_id=1, replica_groups={{256,288,320,352,384,416,448,480,0,32,64,96,128,160,192,224},{257,289,3..., dimensions={0} | all-to-all | bytes 32768 | tf_op jit(solution)/shard_map/all_to_all | solution.py:379
  56.9 0.6 %reduce_sum.19 = f32[2,128]{1,0:T(2,128)} reduce(f32[16,2,128]{2,1,0:T(2,128)S(1)} %all_to_all.16, f32[]{:T(128)} %constant.9.clone.1), dimensions={0}, to_apply=%region_1.2 | reduce | flops 3840 | bytes 17412 | tf_op jit(solution)/shard_map/reduce_sum | solution.py:387
  (1 shorter events, 0.0 us)
Async XLA Ops:
  1.3 27.1 %all-to-all-start = ((bf16[64,2,12]{2,1,0:T(2,128)(2,1)}), bf16[64,2,12]{2,1,0:T(2,128)(2,1)S(1)}, u32[]{:S(2)}, u32[]{:S(2)}) async-start(bf16[64,2,12]{2,1,0:T(2,128)(2,1)} %broadcast_in_dim.2), calls=%async_computation | async-start | bytes 65536 | tf_op jit(solution)/shard_map/all_to_all | solution.py:298

commit v5 on v4

--- a/solution.py
+++ b/solution.py
@@ -110,8 +110,6 @@
     right_ref,
     cell_row,
     cells,
-    vis_rows,
-    uv_rows,
     screen_a,
     screen_b,
     arrival,
@@ -145,8 +143,6 @@
     chosen_ref[...] = jnp.where(chosen & alive, 1.0, 0.0).astype(bf16)
 
     make_shifts(left_ref, right_ref)
-    vis_rows[...] = packed_ref[: 2 * DEVICE_SLOTS, :]
-    uv_rows[...] = packed_ref[2 * DEVICE_SLOTS : 4 * DEVICE_SLOTS, :]
 
     lane = lax.broadcasted_iota(jnp.int32, (S, 2 * S), 1)
     a = (lax.broadcasted_iota(jnp.int32, (S, 2 * S), 0) - S // 2).astype(f32) * (FIELD_WIDTH / S)
@@ -173,10 +169,10 @@
     coarse = (lax.broadcasted_iota(jnp.int32, (8, 1), 0) - 4).astype(f32) * (8.0 / S)
 
     def one_block(b):
-        u = uv_rows[pl.ds(2 * b, 1), :]
-        v = uv_rows[pl.ds(2 * b + 1, 1), :]
-        vr = vis_rows[pl.ds(2 * b, 1), :]
-        vi = vis_rows[pl.ds(2 * b + 1, 1), :]
+        u = packed_ref[pl.ds(2 * DEVICE_SLOTS + 2 * b, 1), :]
+        v = packed_ref[pl.ds(2 * DEVICE_SLOTS + 2 * b + 1, 1), :]
+        vr = packed_ref[pl.ds(2 * b, 1), :]
+        vi = packed_ref[pl.ds(2 * b + 1, 1), :]
         turns = jnp.concatenate([u * fine, u * coarse, v * fine, v * coarse], axis=0)
         c, s = cos_sin_turns(turns)
         cu, su, cua, sua = c[0:8], s[0:8], c[8:16], s[8:16]
@@ -220,15 +216,13 @@
     phase_ref, chosen_ref, touch_ref, left_ref, right_ref, towers_ref, out_ref, facet_ref, rows_ref
 ):
     columns = DEVICE_COLUMNS * N_COL
-    named = touch_ref[...].astype(f32)
-    facet_lane = lax.broadcasted_iota(jnp.int32, (columns, FACETS), 1).astype(f32)
-    touched = named[:, 0:1] == facet_lane
+    named = touch_ref[...].astype(f32).T
+    facet = lax.broadcasted_iota(jnp.int32, (FACETS, columns), 0).astype(f32)
+    touched = named[0:1] == facet
     for t in range(1, TOUCH):
-        touched = touched | (named[:, t : t + 1] == facet_lane)
+        touched = touched | (named[t : t + 1] == facet)
     touched = jnp.where(touched, 1.0, 0.0).astype(bf16)
-    mask = lax.dot_general(
-        touched, chosen_ref[...], (((0,), (0,)), ((), ())), preferred_element_type=f32
-    )
+    mask = jnp.dot(touched, chosen_ref[...], preferred_element_type=f32)
     weights = phase_ref[...] * jnp.concatenate([mask, mask], axis=0)
     high, low = split_bf16(weights)
     left = jnp.concatenate(
@@ -279,7 +273,7 @@
                 rows_ref[pl.ds(2 * place + i, GROUP, stride=GROUP), :] = image[
                     GROUP * i : GROUP * (i + 1), 2 * S * fy : 2 * S * (fy + 1)
                 ]
-    out_ref[...] = rows_ref[...].astype(bf16).reshape(GROUP, GROUP, 2 * S)
+    out_ref[...] = rows_ref[: FACETS * S].astype(bf16).reshape(GROUP, GROUP, 2 * S)
 
 
 VMEM = pl.BlockSpec(memory_space=pltpu.VMEM)
@@ -323,7 +317,7 @@
     towers, phases, chosen, left, right = pl.pallas_call(
         grid_kernel,
         out_shape=(
-            jax.ShapeDtypeStruct((S * DEVICE_SLOTS, 2 * S), f32),
+            jax.ShapeDtypeStruct(((S + 1) * DEVICE_SLOTS, 2 * S), f32),
             jax.ShapeDtypeStruct((2 * FACETS, DEVICE_SLOTS), f32),
             jax.ShapeDtypeStruct((DEVICE_COLUMNS * N_COL, DEVICE_SLOTS), bf16),
             jax.ShapeDtypeStruct((4, 2 * S, 2 * S), bf16),
@@ -334,8 +328,6 @@
         scratch_shapes=[
             pltpu.VMEM((8, BLOCK_VISIBILITY), jnp.int32),
             pltpu.SMEM((8, BLOCK_VISIBILITY), jnp.int32),
-            pltpu.VMEM((2 * DEVICE_SLOTS, BLOCK_VISIBILITY), f32),
-            pltpu.VMEM((2 * DEVICE_SLOTS, BLOCK_VISIBILITY), f32),
             pltpu.VMEM((RANGE_PLANES, S, 2 * S), f32),
             pltpu.VMEM((RANGE_PLANES, S, 2 * S), f32),
             pltpu.SemaphoreType.DMA,
@@ -354,8 +346,8 @@
         in_specs=[VMEM] * 6,
         out_specs=VMEM,
         scratch_shapes=[
-            pltpu.VMEM((FACETS * S, 2 * S), f32),
-            pltpu.VMEM((FACETS * S, 2 * S), f32),
+            pltpu.VMEM((FACETS * S + S, 2 * S), f32),
+            pltpu.VMEM((FACETS * S + GROUP, 2 * S), f32),
         ],
         compiler_params=pltpu.CompilerParams(vmem_limit_bytes=24 * 1024 * 1024),
         name="facet_sums",

time: 58.2 us -> 57.9 us (level)
  no operation moved by 1% of the time
where the time goes in v5:
time: 57.9 us; the launch traced here: 57.3 us
  blocking collectives  26.5 us (46%)
  starting transfers between devices  20.1 us (35%)
  Pallas kernels  7.3 us (13%)
  other arithmetic  2.14 us (4%)
  between operations  0.69 us (1%)
  local copies, waits for them, and re-layouts  0.62 us (1%)
    all_to_all x1, starting transfers between devices, shards(): lax.all_to_all(jnp.broadcast_to(touch_lists[None].astype(bf16), (N_COL, D...  20.1 us
    all_to_all x1, blocking collectives, shards(): lax.all_to_all(plane_rows.reshape(FACETS, 2, 2 * S), 'z', split_axis=0, c...  13.4 us
    all_to_all x1, blocking collectives, shards(): lax.all_to_all(partial_rows, ('x', 'wa'), split_axis=0, concat_axis=0, ax...  13.1 us
    pallas_call x1, Pallas kernels, shards(): pl.pallas_call(grid_kernel, out_shape=(jax.ShapeDtypeStruct(((S + 1) * DE...  5.53 us
    pallas_call x1, Pallas kernels, shards(): pl.pallas_call(facet_kernel, out_shape=jax.ShapeDtypeStruct((GROUP, GROUP...  1.77 us
  transfers between devices with their start and end apart: 1, of which 0 were waited for; matrix products, arithmetic and copies ran while one was open for 1% of the time, Pallas kernels for 10%

profile of v5, /device:TPU:1, one launch (start us, length us, event | category | flops | bytes accessed | tf_op | source)
XLA Modules:
  0.0 57.3 jit_solution(4897568712650099150)
XLA Ops:
  0.0 0.7 %convert_element_type.35 = bf16[2,12]{1,0:T(2,128)(2,1)S(1)} convert(s32[2,12]{1,0:T(2,128)} %param.11) | non-fusion elementwise | flops 24 | bytes 144 | tf_op jit(solution)/shard_map/convert_element_type | solution.py:293
  0.7 0.6 %broadcast_in_dim.2 = bf16[64,2,12]{2,1,0:T(2,128)(2,1)} broadcast(bf16[2,12]{1,0:T(2,128)(2,1)S(1)} %convert_element_type.35), dimensions={1,2} | broadcast | bytes 3120 | tf_op jit(solution)/shard_map/broadcast_in_dim | solution.py:293
  1.3 20.1 %all-to-all-start = ((bf16[64,2,12]{2,1,0:T(2,128)(2,1)}), bf16[64,2,12]{2,1,0:T(2,128)(2,1)S(1)}, u32[]{:S(2)}, u32[]{:S(2)}) async-start(bf16[64,2,12]{2,1,0:T(2,128)(2,1)} %broadcast_in_dim.2), calls=%async_computation | async-start | bytes 65536 | tf_op jit(solution)/shard_map/all_to_all | solution.py:292
  22.1 0.8 %convert_add_fusion.packed_ref = f32[264,128]{1,0:T(8,128)S(1)} fusion(s32[1,1]{1,0:T(1,128)} %bitcast.4, s32[1,1]{1,0:T(1,128)S(6)} %copy.9, s32[1,64]{1,0:T(1,128)} %bitcast.11, s32[1,64]{1,0:T(1,128)} %bitcast.12, bf16[128,128]{1,0:T(8,128)(2,1)} %bitcast.9, bf16[128,128]{1,0:T(8,128)(2,1)} %bitcast.10), kind=kLoop, calls=%fused_computation.1 | loop fusion | flops 371712 | bytes 201224 | tf_op jit(solution)/shard_map/add | solution.py:305
  22.9 5.5 %grid_blocks.1 = (f32[4160,128]{1,0:T(8,128)S(1)}, f32[32,64]{1,0:T(8,128)S(1)}, bf16[128,64]{1,0:T(8,128)(2,1)S(1)}, bf16[4,128,128]{2,1,0:T(8,128)(2,1)S(1)}, bf16[4,128,256]{2,1,0:T(8,128)(2,1)S(1)}) custom-call(f32[264,128]{1,0:T(8,128)S(1)} %convert_add_fusion.packed_ref), custom_call_target="tpu_custom_call" | custom-call | flops 300000000 | bytes 2200000 | tf_op jit(solution)/shard_map/grid_blocks/pallas_call | solution.py:317
  28.4 0.0 all-to-all-done
  28.4 1.8 %facet_sums.1 = bf16[32,32,128]{2,1,0:T(8,128)(2,1)S(1)} custom-call(f32[32,64]{1,0:T(8,128)S(1)} %get-tuple-element.10.phase_ref, bf16[128,64]{1,0:T(8,128)(2,1)S(1)} %get-tuple-element.11.chosen_ref, bf16[128,12]{1,0:T(8,128)(2,1)S(1)} %bitcast.7, bf16[4,128,128]{2,1,0:T(8,128)(2,1)S(1)} %get-tuple-element.12.left_ref, ...), custom_call_target="tpu_custom_call" | custom-call | tf_op jit(solution)/shard_map/facet_sums/pallas_call | solution.py:343
  30.2 13.1 %all_to_all.15 = bf16[32,32,128]{2,1,0:T(8,128)(2,1)S(1)} all-to-all(bf16[32,32,128]{2,1,0:T(8,128)(2,1)S(1)} %facet_sums.1), channel_id=1, replica_groups={{20,21,22,23,16,17,18,19,28,29,30,31,24,25,26,27,4,5,6,7,0,1,2,3,12,13,..., dimensions={0} | all-to-all | bytes 524288 | tf_op jit(solution)/shard_map/all_to_all | solution.py:362
  43.3 13.4 %all_to_all.16 = f32[16,2,128]{2,1,0:T(2,128)S(1)} all-to-all(f32[16,2,128]{2,1,0:T(2,128)S(1)} %bitcast.8), channel_id=1, replica_groups={{256,288,320,352,384,416,448,480,0,32,64,96,128,160,192,224},{257,289,3..., dimensions={0} | all-to-all | bytes 32768 | tf_op jit(solution)/shard_map/all_to_all | solution.py:371
  56.7 0.6 %reduce_sum.19 = f32[2,128]{1,0:T(2,128)} reduce(f32[16,2,128]{2,1,0:T(2,128)S(1)} %all_to_all.16, f32[]{:T(128)} %constant.9.clone.1), dimensions={0}, to_apply=%region_1.2 | reduce | flops 3840 | bytes 17412 | tf_op jit(solution)/shard_map/reduce_sum | solution.py:379
  (1 shorter events, 0.0 us)
Async XLA Ops:
  1.3 27.1 %all-to-all-start = ((bf16[64,2,12]{2,1,0:T(2,128)(2,1)}), bf16[64,2,12]{2,1,0:T(2,128)(2,1)S(1)}, u32[]{:S(2)}, u32[]{:S(2)}) async-start(bf16[64,2,12]{2,1,0:T(2,128)(2,1)} %broadcast_in_dim.2), calls=%async_computation | async-start | bytes 65536 | tf_op jit(solution)/shard_map/all_to_all | solution.py:292

commit v6 on v5

--- a/solution.py
+++ b/solution.py
@@ -25,7 +25,7 @@
 CELL_STEP = 0.37
 WTERM_LIMIT = 4000.0
 SCALE = 1.0 / math.sqrt(BLOCK_VISIBILITY * N_COL * N_WA * DEVICE_SLOTS)
-UNROLL = 8
+UNROLL = 16
 GROUP = 32
 TOUCH_Z, TOUCH_X = 11, 2
 PLANE_X, PLANE_WA = 2, 4
@@ -139,8 +139,7 @@
     place = ((owner // 4 + 16 - TOUCH_Z) % 16) * 4 + (owner + 4 - TOUCH_X) % 4
     place = place * DEVICE_COLUMNS + column_half
     chosen = lax.broadcasted_iota(jnp.int32, (columns, DEVICE_SLOTS), 0) == place
-    alive = lax.broadcasted_iota(jnp.int32, (1, DEVICE_SLOTS), 1) < labels[2:3, 0:1]
-    chosen_ref[...] = jnp.where(chosen & alive, 1.0, 0.0).astype(bf16)
+    chosen_ref[...] = jnp.where(chosen, 1.0, 0.0).astype(bf16)
 
     make_shifts(left_ref, right_ref)
 
@@ -151,7 +150,7 @@
     lag = -radius / (1.0 + jnp.sqrt(1.0 - radius))
     sign = jnp.where(lane < S, -1.0, 1.0).astype(f32)
     plane_step = 2.0 * WTERM_LIMIT / (RANGE_PLANES * N_WA)
-    first_plane = (labels[3:4, 0:1] * RANGE_PLANES).astype(f32)
+    first_plane = (labels[2:3, 0:1] * RANGE_PLANES).astype(f32)
     first_turns = (-WTERM_LIMIT + (first_plane + 0.5) * plane_step) * lag
     step_turns = plane_step * lag
 
@@ -213,7 +212,7 @@
 
 
 def facet_kernel(
-    phase_ref, chosen_ref, touch_ref, left_ref, right_ref, towers_ref, out_ref, facet_ref, rows_ref
+    live_ref, phase_ref, chosen_ref, touch_ref, left_ref, right_ref, towers_ref, out_ref, facet_ref, rows_ref
 ):
     columns = DEVICE_COLUMNS * N_COL
     named = touch_ref[...].astype(f32).T
@@ -223,6 +222,8 @@
         touched = touched | (named[t : t + 1] == facet)
     touched = jnp.where(touched, 1.0, 0.0).astype(bf16)
     mask = jnp.dot(touched, chosen_ref[...], preferred_element_type=f32)
+    slot = lax.broadcasted_iota(jnp.int32, (FACETS, DEVICE_SLOTS), 1)
+    mask = jnp.where(slot < live_ref[...], mask, 0.0)
     weights = phase_ref[...] * jnp.concatenate([mask, mask], axis=0)
     high, low = split_bf16(weights)
     left = jnp.concatenate(
@@ -308,10 +309,9 @@
         ).astype(f32)
         + jnp.pad(cells, ((2 * half, 7), lanes)).astype(f32)
         + jnp.pad(block_owner_index.reshape(1, DEVICE_SLOTS), ((2 * half + 1, 6), lanes)).astype(f32)
-        + jnp.pad(live_counts, ((2 * half + 2, 5), (0, BLOCK_VISIBILITY - 1))).astype(f32)
         + jnp.pad(
             range_index.reshape(1, 1).astype(jnp.int32),
-            ((2 * half + 3, 4), (0, BLOCK_VISIBILITY - 1)),
+            ((2 * half + 2, 5), (0, BLOCK_VISIBILITY - 1)),
         ).astype(f32)
     )
     towers, phases, chosen, left, right = pl.pallas_call(
@@ -343,7 +343,7 @@
     partial_rows = pl.pallas_call(
         facet_kernel,
         out_shape=jax.ShapeDtypeStruct((GROUP, GROUP, 2 * S), bf16),
-        in_specs=[VMEM] * 6,
+        in_specs=[VMEM] * 7,
         out_specs=VMEM,
         scratch_shapes=[
             pltpu.VMEM((FACETS * S + S, 2 * S), f32),
@@ -352,6 +352,7 @@
         compiler_params=pltpu.CompilerParams(vmem_limit_bytes=24 * 1024 * 1024),
         name="facet_sums",
     )(
+        live_counts,
         phases,
         chosen,
         named,

time: 57.9 us -> 57.9 us (level)
  no operation moved by 1% of the time
where the time goes in v6:
time: 57.9 us; the launch traced here: 57.2 us
  blocking collectives  26.5 us (46%)
  starting transfers between devices  20.1 us (35%)
  Pallas kernels  7.21 us (12%)
  other arithmetic  2.14 us (4%)
  between operations  0.69 us (1%)
  local copies, waits for them, and re-layouts  0.62 us (1%)
    all_to_all x1, starting transfers between devices, shards(): lax.all_to_all(jnp.broadcast_to(touch_lists[None].astype(bf16), (N_COL, D...  20.1 us
    all_to_all x1, blocking collectives, shards(): lax.all_to_all(plane_rows.reshape(FACETS, 2, 2 * S), 'z', split_axis=0, c...  13.4 us
    all_to_all x1, blocking collectives, shards(): lax.all_to_all(partial_rows, ('x', 'wa'), split_axis=0, concat_axis=0, ax...  13.1 us
    pallas_call x1, Pallas kernels, shards(): pl.pallas_call(grid_kernel, out_shape=(jax.ShapeDtypeStruct(((S + 1) * DE...  5.44 us
    pallas_call x1, Pallas kernels, shards(): pl.pallas_call(facet_kernel, out_shape=jax.ShapeDtypeStruct((GROUP, GROUP...  1.77 us
  transfers between devices with their start and end apart: 1, of which 0 were waited for; matrix products, arithmetic and copies ran while one was open for 1% of the time, Pallas kernels for 10%

profile of v6, /device:TPU:1, one launch (start us, length us, event | category | flops | bytes accessed | tf_op | source)
XLA Modules:
  0.0 57.2 jit_solution(1431375072089260925)
XLA Ops:
  0.0 0.7 %convert_element_type.31 = bf16[2,12]{1,0:T(2,128)(2,1)S(1)} convert(s32[2,12]{1,0:T(2,128)} %param.11) | non-fusion elementwise | flops 24 | bytes 144 | tf_op jit(solution)/shard_map/convert_element_type | solution.py:294
  0.7 0.6 %broadcast_in_dim.2 = bf16[64,2,12]{2,1,0:T(2,128)(2,1)} broadcast(bf16[2,12]{1,0:T(2,128)(2,1)S(1)} %convert_element_type.31), dimensions={1,2} | broadcast | bytes 3120 | tf_op jit(solution)/shard_map/broadcast_in_dim | solution.py:294
  1.3 20.1 %all-to-all-start = ((bf16[64,2,12]{2,1,0:T(2,128)(2,1)}), bf16[64,2,12]{2,1,0:T(2,128)(2,1)S(1)}, u32[]{:S(2)}, u32[]{:S(2)}) async-start(bf16[64,2,12]{2,1,0:T(2,128)(2,1)} %broadcast_in_dim.2), calls=%async_computation | async-start | bytes 65536 | tf_op jit(solution)/shard_map/all_to_all | solution.py:293
  21.4 0.8 %convert_add_fusion.packed_ref = f32[264,128]{1,0:T(8,128)S(1)} fusion(s32[1,1]{1,0:T(1,128)} %bitcast.4, s32[1,64]{1,0:T(1,128)} %bitcast.11, s32[1,64]{1,0:T(1,128)} %bitcast.12, bf16[128,128]{1,0:T(8,128)(2,1)} %bitcast.9, bf16[128,128]{1,0:T(8,128)(2,1)} %bitcast.10), kind=kLoop, calls=%fused_computation.1 | loop fusion | flops 304128 | bytes 201220 | tf_op jit(solution)/shard_map/add | solution.py:306
  22.2 5.4 %grid_blocks.1 = (f32[4160,128]{1,0:T(8,128)S(1)}, f32[32,64]{1,0:T(8,128)S(1)}, bf16[128,64]{1,0:T(8,128)(2,1)S(1)}, bf16[4,128,128]{2,1,0:T(8,128)(2,1)S(1)}, bf16[4,128,256]{2,1,0:T(8,128)(2,1)S(1)}) custom-call(f32[264,128]{1,0:T(8,128)S(1)} %convert_add_fusion.packed_ref), custom_call_target="tpu_custom_call" | custom-call | flops 300000000 | bytes 2200000 | tf_op jit(solution)/shard_map/grid_blocks/pallas_call | solution.py:317
  28.3 0.0 all-to-all-done
  28.3 1.8 %facet_sums.1 = bf16[32,32,128]{2,1,0:T(8,128)(2,1)S(1)} custom-call(s32[1,1]{1,0:T(1,128)S(6)} %copy.9.live_ref, f32[32,64]{1,0:T(8,128)S(1)} %get-tuple-element.10.phase_ref, bf16[128,64]{1,0:T(8,128)(2,1)S(1)} %get-tuple-element.11.chosen_ref, bf16[128,12]{1,0:T(8,128)(2,1)S(1)} %bitcast.7, bf16[4,128,128]{2,1,0:T(8,128)(2,1)S(1)} %get-tuple-element.12.left_ref, ...), custom_call_target="tpu_custom_call" | custom-call | tf_op jit(solution)/shard_map/facet_sums/pallas_call | solution.py:343
  30.1 13.1 %all_to_all.15 = bf16[32,32,128]{2,1,0:T(8,128)(2,1)S(1)} all-to-all(bf16[32,32,128]{2,1,0:T(8,128)(2,1)S(1)} %facet_sums.1), channel_id=1, replica_groups={{20,21,22,23,16,17,18,19,28,29,30,31,24,25,26,27,4,5,6,7,0,1,2,3,12,13,..., dimensions={0} | all-to-all | bytes 524288 | tf_op jit(solution)/shard_map/all_to_all | solution.py:363
  43.2 13.4 %all_to_all.16 = f32[16,2,128]{2,1,0:T(2,128)S(1)} all-to-all(f32[16,2,128]{2,1,0:T(2,128)S(1)} %bitcast.8), channel_id=1, replica_groups={{256,288,320,352,384,416,448,480,0,32,64,96,128,160,192,224},{257,289,3..., dimensions={0} | all-to-all | bytes 32768 | tf_op jit(solution)/shard_map/all_to_all | solution.py:372
  56.6 0.6 %reduce_sum.19 = f32[2,128]{1,0:T(2,128)} reduce(f32[16,2,128]{2,1,0:T(2,128)S(1)} %all_to_all.16, f32[]{:T(128)} %constant.9.clone.1), dimensions={0}, to_apply=%region_1.2 | reduce | flops 3840 | bytes 17412 | tf_op jit(solution)/shard_map/reduce_sum | solution.py:380
  (1 shorter events, 0.0 us)
Async XLA Ops:
  1.3 27.0 %all-to-all-start = ((bf16[64,2,12]{2,1,0:T(2,128)(2,1)}), bf16[64,2,12]{2,1,0:T(2,128)(2,1)S(1)}, u32[]{:S(2)}, u32[]{:S(2)}) async-start(bf16[64,2,12]{2,1,0:T(2,128)(2,1)} %broadcast_in_dim.2), calls=%async_computation | async-start | bytes 65536 | tf_op jit(solution)/shard_map/all_to_all | solution.py:293

commit v7 on v6

--- a/solution.py
+++ b/solution.py
@@ -27,7 +27,7 @@
 SCALE = 1.0 / math.sqrt(BLOCK_VISIBILITY * N_COL * N_WA * DEVICE_SLOTS)
 UNROLL = 16
 GROUP = 32
-TOUCH_Z, TOUCH_X = 11, 2
+TOUCH_Z, TOUCH_X = 11, 0
 PLANE_X, PLANE_WA = 2, 4
 LINE_Z = 8
 

time: 57.9 us -> 58 us (level)
  starting transfers between devices: 20.1 us -> 19.4 us
  blocking collectives: 26.5 us -> 27.2 us
    all_to_all x1, blocking collectives: 13.1 us -> 13.9 us  [shards(): lax.all_to_all(partial_rows, ('x', 'wa'), split_axis=0, concat_axis=0, ax...]
    all_to_all x1, starting transfers between devices: 20.1 us -> 19.4 us  [shards(): lax.all_to_all(jnp.broadcast_to(touch_lists[None].astype(bf16), (N_COL, D...]
  transfers between devices with their start and end apart: 1 -> 1, of which waited for: 0 -> 0; matrix products, arithmetic and copies ran while one was open for 1% -> 1% of each run, Pallas kernels for 10% -> 9%
where the time goes in v7:
time: 58 us; the launch traced here: 57.3 us
  blocking collectives  27.2 us (47%)
  starting transfers between devices  19.4 us (33%)
  Pallas kernels  7.2 us (12%)
  other arithmetic  2.14 us (4%)
  between operations  0.68 us (1%)
  local copies, waits for them, and re-layouts  0.62 us (1%)
    all_to_all x1, starting transfers between devices, shards(): lax.all_to_all(jnp.broadcast_to(touch_lists[None].astype(bf16), (N_COL, D...  19.4 us
    all_to_all x1, blocking collectives, shards(): lax.all_to_all(partial_rows, ('x', 'wa'), split_axis=0, concat_axis=0, ax...  13.9 us
    all_to_all x1, blocking collectives, shards(): lax.all_to_all(plane_rows.reshape(FACETS, 2, 2 * S), 'z', split_axis=0, c...  13.3 us
    pallas_call x1, Pallas kernels, shards(): pl.pallas_call(grid_kernel, out_shape=(jax.ShapeDtypeStruct(((S + 1) * DE...  5.43 us
    pallas_call x1, Pallas kernels, shards(): pl.pallas_call(facet_kernel, out_shape=jax.ShapeDtypeStruct((GROUP, GROUP...  1.77 us
  transfers between devices with their start and end apart: 1, of which 0 were waited for; matrix products, arithmetic and copies ran while one was open for 1% of the time, Pallas kernels for 9%

profile of v7, /device:TPU:1, one launch (start us, length us, event | category | flops | bytes accessed | tf_op | source)
XLA Modules:
  0.0 57.3 jit_solution(12042749801516060658)
XLA Ops:
  0.0 0.7 %convert_element_type.31 = bf16[2,12]{1,0:T(2,128)(2,1)S(1)} convert(s32[2,12]{1,0:T(2,128)} %param.11) | non-fusion elementwise | flops 24 | bytes 144 | tf_op jit(solution)/shard_map/convert_element_type | solution.py:294
  0.7 0.6 %broadcast_in_dim.2 = bf16[64,2,12]{2,1,0:T(2,128)(2,1)} broadcast(bf16[2,12]{1,0:T(2,128)(2,1)S(1)} %convert_element_type.31), dimensions={1,2} | broadcast | bytes 3120 | tf_op jit(solution)/shard_map/broadcast_in_dim | solution.py:294
  1.3 19.4 %all-to-all-start = ((bf16[64,2,12]{2,1,0:T(2,128)(2,1)}), bf16[64,2,12]{2,1,0:T(2,128)(2,1)S(1)}, u32[]{:S(2)}, u32[]{:S(2)}) async-start(bf16[64,2,12]{2,1,0:T(2,128)(2,1)} %broadcast_in_dim.2), calls=%async_computation | async-start | bytes 65536 | tf_op jit(solution)/shard_map/all_to_all | solution.py:293
  20.8 0.8 %convert_add_fusion.packed_ref = f32[264,128]{1,0:T(8,128)S(1)} fusion(s32[1,1]{1,0:T(1,128)} %bitcast.4, s32[1,64]{1,0:T(1,128)} %bitcast.11, s32[1,64]{1,0:T(1,128)} %bitcast.12, bf16[128,128]{1,0:T(8,128)(2,1)} %bitcast.9, bf16[128,128]{1,0:T(8,128)(2,1)} %bitcast.10), kind=kLoop, calls=%fused_computation.1 | loop fusion | flops 304128 | bytes 201220 | tf_op jit(solution)/shard_map/add | solution.py:306
  21.6 5.4 %grid_blocks.1 = (f32[4160,128]{1,0:T(8,128)S(1)}, f32[32,64]{1,0:T(8,128)S(1)}, bf16[128,64]{1,0:T(8,128)(2,1)S(1)}, bf16[4,128,128]{2,1,0:T(8,128)(2,1)S(1)}, bf16[4,128,256]{2,1,0:T(8,128)(2,1)S(1)}) custom-call(f32[264,128]{1,0:T(8,128)S(1)} %convert_add_fusion.packed_ref), custom_call_target="tpu_custom_call" | custom-call | flops 300000000 | bytes 2200000 | tf_op jit(solution)/shard_map/grid_blocks/pallas_call | solution.py:317
  27.7 0.0 all-to-all-done
  27.7 1.8 %facet_sums.1 = bf16[32,32,128]{2,1,0:T(8,128)(2,1)S(1)} custom-call(s32[1,1]{1,0:T(1,128)S(6)} %copy.9.live_ref, f32[32,64]{1,0:T(8,128)S(1)} %get-tuple-element.10.phase_ref, bf16[128,64]{1,0:T(8,128)(2,1)S(1)} %get-tuple-element.11.chosen_ref, bf16[128,12]{1,0:T(8,128)(2,1)S(1)} %bitcast.7, bf16[4,128,128]{2,1,0:T(8,128)(2,1)S(1)} %get-tuple-element.12.left_ref, ...), custom_call_target="tpu_custom_call" | custom-call | tf_op jit(solution)/shard_map/facet_sums/pallas_call | solution.py:343
  29.5 13.9 %all_to_all.15 = bf16[32,32,128]{2,1,0:T(8,128)(2,1)S(1)} all-to-all(bf16[32,32,128]{2,1,0:T(8,128)(2,1)S(1)} %facet_sums.1), channel_id=1, replica_groups={{20,21,22,23,16,17,18,19,28,29,30,31,24,25,26,27,4,5,6,7,0,1,2,3,12,13,..., dimensions={0} | all-to-all | bytes 524288 | tf_op jit(solution)/shard_map/all_to_all | solution.py:363
  43.4 13.3 %all_to_all.16 = f32[16,2,128]{2,1,0:T(2,128)S(1)} all-to-all(f32[16,2,128]{2,1,0:T(2,128)S(1)} %bitcast.8), channel_id=1, replica_groups={{256,288,320,352,384,416,448,480,0,32,64,96,128,160,192,224},{257,289,3..., dimensions={0} | all-to-all | bytes 32768 | tf_op jit(solution)/shard_map/all_to_all | solution.py:372
  56.7 0.6 %reduce_sum.19 = f32[2,128]{1,0:T(2,128)} reduce(f32[16,2,128]{2,1,0:T(2,128)S(1)} %all_to_all.16, f32[]{:T(128)} %constant.9.clone.1), dimensions={0}, to_apply=%region_1.2 | reduce | flops 3840 | bytes 17412 | tf_op jit(solution)/shard_map/reduce_sum | solution.py:380
  (1 shorter events, 0.0 us)
Async XLA Ops:
  1.3 26.4 %all-to-all-start = ((bf16[64,2,12]{2,1,0:T(2,128)(2,1)}), bf16[64,2,12]{2,1,0:T(2,128)(2,1)S(1)}, u32[]{:S(2)}, u32[]{:S(2)}) async-start(bf16[64,2,12]{2,1,0:T(2,128)(2,1)} %broadcast_in_dim.2), calls=%async_computation | async-start | bytes 65536 | tf_op jit(solution)/shard_map/all_to_all | solution.py:293
